TPU v7x, 512 devices: a whole 4x8x8 slice. The times are simulated.
512 devices in a mesh: fsdp: 32 (over x, y), layer: 8 (over z), own: 2 (over core).
Axes of the slice: x: 4, y: 8, z: 8, core: 2. Of those that a mesh axis runs over, the one named last changes fastest.
Arguments:
- factor: bfloat16 [448, 512, 512], P('layer', ('fsdp', 'own')), as said below
- old_basis: bfloat16 [448, 512, 512], P('layer', ('fsdp', 'own')), as said below
- moment: bfloat16 [448, 1024, 512], P('layer', ('fsdp', 'own')), may hold values from -6 to 6
- owner_table: int32 [448, 1], P('layer'), may hold values from 0 to 63; in each aligned block of 56 rows (0 to 55, 56 to 111, ...) at most 2 rows name the same one
Outputs:
- moment_out: bfloat16 [448, 1024, 512], P('layer', ('fsdp', 'own'))
- owner_basis: bfloat16 [8, 128, 512, 512], P('layer', ('fsdp', 'own'))
Inputs may be any that keep to these rules, and one draw needn't show every extreme that they name: `owner_table`: within each layer group's 56 blocks (the rows of one index of layer), no owner is named more than 2 times, a bound that some block reaches. `factor`: each block is symmetric with a dominant positive diagonal. `old_basis`: each block is the identity plus a dense perturbation, well conditioned but not orthonormal.
All inputs are finite; a program needn't handle non-finite values.
Results may differ from a plain program's by a relative error of at most 0.014.
Values may be sent and summed in bfloat16 or wider, within the bound.
A program may use at most 64 MiB of HBM per device.

v0:
```python
import jax
import jax.numpy as jnp
from jax import lax
from jax.sharding import PartitionSpec as P

SLOTS = 2


def pack(selector, pieces, slot_count):
    share_count = selector.shape[0] // slot_count
    flat = jnp.dot(
        selector, pieces.reshape(pieces.shape[0], -1), preferred_element_type=jnp.float32
    ).astype(jnp.bfloat16)
    return flat.reshape(slot_count, share_count, pieces.shape[1], pieces.shape[2])


def deliver(first, second, third):
    return (
        lax.all_to_all(first, ("fsdp", "own"), split_axis=1, concat_axis=1, tiled=True),
        lax.all_to_all(second, ("fsdp", "own"), split_axis=1, concat_axis=1, tiled=True),
        lax.all_to_all(third, ("fsdp", "own"), split_axis=1, concat_axis=1, tiled=True),
    )


def refresh(factor_slots, basis_slots, moment_slots):
    block_order = factor_slots.shape[-1]
    power = jnp.einsum(
        "bij,bjk->bik", factor_slots, basis_slots, preferred_element_type=jnp.float32
    ).astype(jnp.bfloat16)
    gram_matrix = jnp.einsum("bji,bjk->bik", power, power, preferred_element_type=jnp.float32)
    vacant = (jnp.trace(gram_matrix, axis1=1, axis2=2) == 0.0).astype(jnp.float32)
    identity = jnp.eye(block_order, dtype=jnp.float32)
    gram_matrix = gram_matrix + vacant[:, None, None] * identity[None]
    lower_factor = jnp.linalg.cholesky(gram_matrix)
    fresh_basis = lax.linalg.triangular_solve(
        lower_factor, power.astype(jnp.float32), left_side=False, lower=True, transpose_a=True
    ).astype(jnp.bfloat16)
    rotation = jnp.einsum(
        "bji,bjk->bik", basis_slots, fresh_basis, preferred_element_type=jnp.float32
    ).astype(jnp.bfloat16)
    rotated = jnp.einsum(
        "bcj,bjk->bck", moment_slots, rotation, preferred_element_type=jnp.float32
    ).astype(jnp.bfloat16)
    return (fresh_basis, rotated)


def per_device(factor, old_basis, moment, owner_table):
    shares = lax.axis_size(("fsdp", "own"))
    blocks, row_count, block_order = factor.shape
    col_count = moment.shape[1]
    owners = owner_table[:, 0]
    position = jnp.arange(blocks, dtype=jnp.int32)
    earlier = (owners[None, :] == owners[:, None]) & (position[None, :] < position[:, None])
    slot_rank = jnp.sum(earlier.astype(jnp.int32), axis=1)
    target = slot_rank * shares + owners
    picker = (jnp.arange(SLOTS * shares, dtype=jnp.int32)[:, None] == target[None, :]).astype(
        jnp.bfloat16
    )
    delivered = deliver(
        pack(picker, factor, SLOTS), pack(picker, old_basis, SLOTS), pack(picker, moment, SLOTS)
    )
    fresh_basis, rotated = refresh(
        delivered[0].reshape(SLOTS, block_order, block_order),
        delivered[1].reshape(SLOTS, block_order, block_order),
        delivered[2].reshape(SLOTS, shares * col_count, block_order),
    )
    returned = lax.all_to_all(
        rotated.reshape(SLOTS, shares, col_count, block_order),
        ("fsdp", "own"),
        split_axis=1,
        concat_axis=1,
        tiled=True,
    )
    gathered = jnp.einsum(
        "kb,kx->bx",
        picker,
        returned.reshape(SLOTS * shares, -1),
        preferred_element_type=jnp.float32,
    )
    moment_out = gathered.astype(jnp.bfloat16).reshape(blocks, col_count, block_order)
    owner_basis = fresh_basis[None]
    return (moment_out, owner_basis)


def solution(mesh):
    in_specs = (
        P("layer", ("fsdp", "own"), None),
        P("layer", ("fsdp", "own"), None),
        P("layer", ("fsdp", "own"), None),
        P("layer", None),
    )
    out_specs = (P("layer", ("fsdp", "own"), None), P("layer", ("fsdp", "own"), None, None))
    return jax.shard_map(
        per_device, mesh=mesh, in_specs=in_specs, out_specs=out_specs, check_vma=False
    )
```

profile of v0, /device:TPU:1, one launch (start us, length us, event | category | flops | bytes accessed | tf_op | source)
XLA Modules:
  0.0 456.1 jit_solution(4172960511955024637)
XLA Ops:
  5.3 11.6 %all-to-all-start.1 = ((bf16[2,64,8,512]{3,2,0,1:T(8,128)(2,1)}), bf16[2,64,8,512]{3,2,0,1:T(8,128)(2,1)S(1)}, u32[]{:S(2)}, u32[]{:S(2)}) async-start(bf16[2,64,8,512]{3,2,0,1:T(8,128)(2,1)} %copy.70), calls=%async_computation.1 | async-start | bytes 2097152 | tf_op jit(solution)/shard_map/all_to_all | solution.py:20
  19.1 26.4 %all-to-all-done.1 = bf16[2,64,8,512]{3,2,0,1:T(8,128)(2,1)S(1)} async-done(((bf16[2,64,8,512]{3,2,0,1:T(8,128)(2,1)}), bf16[2,64,8,512]{3,2,0,1:T(8,128)(2,1)S(1)}, u32[]{:S(2)}, u32[]{:S(2)}) %all-to-all-start.1) | async-done | bytes 1048608 | tf_op jit(solution)/shard_map/all_to_all | solution.py:20
  45.5 6.2 %all-to-all-start.2 = ((bf16[2,64,8,512]{3,2,0,1:T(8,128)(2,1)}), bf16[2,64,8,512]{3,2,0,1:T(8,128)(2,1)S(1)}, u32[]{:S(2)}, u32[]{:S(2)}) async-start(bf16[2,64,8,512]{3,2,0,1:T(8,128)(2,1)} %copy.72), calls=%async_computation.2 | async-start | bytes 2097152 | tf_op jit(solution)/shard_map/all_to_all | solution.py:19
  60.2 20.1 %all-to-all-done.2 = bf16[2,64,8,512]{3,2,0,1:T(8,128)(2,1)S(1)} async-done(((bf16[2,64,8,512]{3,2,0,1:T(8,128)(2,1)}), bf16[2,64,8,512]{3,2,0,1:T(8,128)(2,1)S(1)}, u32[]{:S(2)}, u32[]{:S(2)}) %all-to-all-start.2) | async-done | bytes 1048608 | tf_op jit(solution)/shard_map/all_to_all | solution.py:19
  80.3 6.7 %all-to-all-start = ((bf16[2,64,16,512]{3,2,0,1:T(8,128)(2,1)}), bf16[2,64,16,512]{3,2,0,1:T(8,128)(2,1)}, u32[]{:S(2)}, u32[]{:S(2)}) async-start(bf16[2,64,16,512]{3,2,0,1:T(8,128)(2,1)} %copy.68), calls=%async_computation | async-start | bytes 4194304 | tf_op jit(solution)/shard_map/all_to_all | solution.py:21
  92.0 3.0 fusion.1
  96.4 23.5 %custom-call.34 = f32[2,128,128]{2,1,0:T(8,128)S(1)} custom-call(f32[2,128,128]{2,1,0:T(8,128)S(1)} %cholesky.271), custom_call_target="Cholesky" | custom-call | tf_op jit(solution)/shard_map/jit(cholesky)/cholesky | solution.py:34
  119.9 19.7 %custom-call.35 = f32[2,1,128,128]{2,3,1,0:T(8,128)S(1)} custom-call(f32[2,1,128,128]{3,2,1,0:T(8,128)S(1)} %select_bitcast_fusion.2), custom_call_target="InvertDiagBlocksLowerTriangular" | custom-call | tf_op jit(solution)/shard_map/jit(cholesky)/cholesky | solution.py:34
  143.5 25.1 %custom-call.36 = f32[2,128,128]{2,1,0:T(8,128)} custom-call(f32[2,128,128]{2,1,0:T(8,128)} %cholesky.275), custom_call_target="Cholesky" | custom-call | tf_op jit(solution)/shard_map/jit(cholesky)/cholesky | solution.py:34
  170.2 21.1 %custom-call.37 = f32[2,1,128,128]{2,3,1,0:T(8,128)} custom-call(f32[2,1,128,128]{3,2,1,0:T(8,128)} %get-tuple-element.35), custom_call_target="InvertDiagBlocksLowerTriangular" | custom-call | tf_op jit(solution)/shard_map/jit(cholesky)/cholesky | solution.py:34
  194.8 24.9 %custom-call.38 = f32[2,128,128]{2,1,0:T(8,128)} custom-call(f32[2,128,128]{2,1,0:T(8,128)} %cholesky.280), custom_call_target="Cholesky" | custom-call | tf_op jit(solution)/shard_map/jit(cholesky)/cholesky | solution.py:34
  221.3 21.5 %custom-call.39 = f32[2,1,128,128]{2,3,1,0:T(8,128)} custom-call(f32[2,1,128,128]{3,2,1,0:T(8,128)} %get-tuple-element.33), custom_call_target="InvertDiagBlocksLowerTriangular" | custom-call | tf_op jit(solution)/shard_map/jit(cholesky)/cholesky | solution.py:34
  245.4 23.5 %custom-call.40 = f32[2,128,128]{2,1,0:T(8,128)S(1)} custom-call(f32[2,128,128]{2,1,0:T(8,128)S(1)} %convolution_subtract_fusion.4), custom_call_target="Cholesky" | custom-call | tf_op jit(solution)/shard_map/jit(cholesky)/cholesky | solution.py:34
  273.1 14.5 %while.1 = (s32[]{:T(128)}, f32[2,512,512]{2,1,0:T(8,128)}, s32[4,2]{0,1:T(2,128)S(1)}, f32[4,2,128,128]{3,2,0,1:T(8,128)}, s32[]{:T(128)}) while((s32[]{:T(128)}, f32[2,512,512]{2,1,0:T(8,128)}, s32[4,2]{0,1:T(2,128)S(1)}, f32[4,2,128,128]{3,2,0,1:T(8,128)}, s32[]{:T(128)}) %tuple.40), condition=%wide.while_cond, body=%wide.while_body.sunk | while | flops 2 | bytes 263777 | solution.py:35
  273.8 3.0 bitcast_dynamic-update-slice_fusion.2
  277.4 3.0 bitcast_dynamic-update-slice_fusion.2
  281.1 3.0 bitcast_dynamic-update-slice_fusion.2
  284.7 3.0 bitcast_dynamic-update-slice_fusion.2
  287.7 79.6 %custom-call.41 = f32[2,4,128,128]{2,3,1,0:T(8,128)S(1)} custom-call(f32[2,4,128,128]{3,2,1,0:T(8,128)} %bitcast.135), custom_call_target="InvertDiagBlocksLowerTriangular" | custom-call | tf_op jit(solution)/shard_map/triangular_solve | solution.py:35
  377.1 3.8 fusion.8
  383.3 4.3 convolution_convert_fusion.4
  387.6 3.2 copy.92
  390.7 10.6 %all-to-all-start.3 = ((bf16[2,64,16,512]{3,2,0,1:T(8,128)(2,1)}), bf16[2,64,16,512]{3,2,0,1:T(8,128)(2,1)S(1)}, u32[]{:S(2)}, u32[]{:S(2)}) async-start(bf16[2,64,16,512]{3,2,0,1:T(8,128)(2,1)} %copy.92), calls=%async_computation.3 | async-start | bytes 4194304 | tf_op jit(solution)/shard_map/all_to_all | solution.py:67
  403.9 48.6 %all-to-all-done.3 = bf16[2,64,16,512]{3,2,0,1:T(8,128)(2,1)S(1)} async-done(((bf16[2,64,16,512]{3,2,0,1:T(8,128)(2,1)}), bf16[2,64,16,512]{3,2,0,1:T(8,128)(2,1)S(1)}, u32[]{:S(2)}, u32[]{:S(2)}) %all-to-all-start.3) | async-done | bytes 2097184 | tf_op jit(solution)/shard_map/all_to_all | solution.py:67
  (86 shorter events, 59.6 us)
Async XLA Ops:
  2.2 51.2 %copy-start.6 = (s32[56]{0:T(128)}, s32[56]{0:T(128)S(1)}, u32[]{:S(2)}) copy-start(s32[56]{0:T(128)S(1)} %multiply_add_fusion) | copy-start | bytes 676
  4.2 12.8 %copy-start.5 = (bf16[56,8,512]{2,1,0:T(8,128)(2,1)S(1)}, bf16[56,8,512]{2,1,0:T(8,128)(2,1)}, u32[]{:S(2)}) copy-start(bf16[56,8,512]{2,1,0:T(8,128)(2,1)} %param.4) | copy-start | bytes 1376260
  5.3 40.2 %all-to-all-start.1 = ((bf16[2,64,8,512]{3,2,0,1:T(8,128)(2,1)}), bf16[2,64,8,512]{3,2,0,1:T(8,128)(2,1)S(1)}, u32[]{:S(2)}, u32[]{:S(2)}) async-start(bf16[2,64,8,512]{3,2,0,1:T(8,128)(2,1)} %copy.70), calls=%async_computation.1 | async-start | bytes 2097152 | tf_op jit(solution)/shard_map/all_to_all | solution.py:20
  45.5 34.8 %all-to-all-start.2 = ((bf16[2,64,8,512]{3,2,0,1:T(8,128)(2,1)}), bf16[2,64,8,512]{3,2,0,1:T(8,128)(2,1)S(1)}, u32[]{:S(2)}, u32[]{:S(2)}) async-start(bf16[2,64,8,512]{3,2,0,1:T(8,128)(2,1)} %copy.72), calls=%async_computation.2 | async-start | bytes 2097152 | tf_op jit(solution)/shard_map/all_to_all | solution.py:19
  80.3 301.2 %all-to-all-start = ((bf16[2,64,16,512]{3,2,0,1:T(8,128)(2,1)}), bf16[2,64,16,512]{3,2,0,1:T(8,128)(2,1)}, u32[]{:S(2)}, u32[]{:S(2)}) async-start(bf16[2,64,16,512]{3,2,0,1:T(8,128)(2,1)} %copy.68), calls=%async_computation | async-start | bytes 4194304 | tf_op jit(solution)/shard_map/all_to_all | solution.py:21
  89.1 1.1 copy-start.2
  95.0 1.3 copy-start.1
  119.8 21.5 %copy-start.3 = (f32[2,128,128]{2,1,0:T(8,128)}, f32[2,128,128]{2,1,0:T(8,128)S(1)}, u32[]{:S(2)}) copy-start(f32[2,128,128]{2,1,0:T(8,128)S(1)} %custom-call.34) | copy-start | bytes 393220
  192.5 76.4 %copy-start.4 = (f32[2,128,128]{2,1,0:T(8,128)S(1)}, f32[2,128,128]{2,1,0:T(8,128)}, u32[]{:S(2)}) copy-start(f32[2,128,128]{2,1,0:T(8,128)} %copy-done.3) | copy-start | bytes 393220
  270.4 2.7 copy-start.8
  367.3 5.7 %copy-start = (f32[2,512,512]{2,1,0:T(8,128)S(1)}, f32[2,512,512]{2,1,0:T(8,128)}, u32[]{:S(2)}) copy-start(f32[2,512,512]{2,1,0:T(8,128)} %get-tuple-element.41) | copy-start | bytes 6291460
  390.7 61.8 %all-to-all-start.3 = ((bf16[2,64,16,512]{3,2,0,1:T(8,128)(2,1)}), bf16[2,64,16,512]{3,2,0,1:T(8,128)(2,1)S(1)}, u32[]{:S(2)}, u32[]{:S(2)}) async-start(bf16[2,64,16,512]{3,2,0,1:T(8,128)(2,1)} %copy.92), calls=%async_computation.3 | async-start | bytes 4194304 | tf_op jit(solution)/shard_map/all_to_all | solution.py:67
  452.7 1.4 copy-start.7
where the time goes:
time: 463 us; the launch traced here: 456 us
  other arithmetic  256 us (55%)
  waiting for transfers between devices  95.1 us (21%)
  local copies, waits for them, and re-layouts  37 us (8%)
  starting transfers between devices  35.2 us (8%)
  matrix products  32 us (7%)
    another operation x18, other arithmetic, refresh(): lower_factor = jnp.linalg.cholesky(gram_matrix)  164 us
    another operation x5, other arithmetic, refresh(): lax.linalg.triangular_solve(lower_factor, power.astype(jnp.float32), left...  84.8 us
    all_to_all x1, waiting for transfers between devices, per_device(): lax.all_to_all(rotated.reshape(SLOTS, shares, col_count, block_order), ('...  48.6 us
    all_to_all x1, waiting for transfers between devices, deliver(): lax.all_to_all(second, ('fsdp', 'own'), split_axis=1, concat_axis=1, tile...  26.4 us
    all_to_all x1, waiting for transfers between devices, deliver(): lax.all_to_all(first, ('fsdp', 'own'), split_axis=1, concat_axis=1, tiled...  20.1 us
    another operation x12, local copies, waits for them, and re-layouts  14.5 us
    another operation x7, matrix products, refresh(): lax.linalg.triangular_solve(lower_factor, power.astype(jnp.float32), left...  14.2 us
    all_to_all x1, starting transfers between devices, deliver(): lax.all_to_all(second, ('fsdp', 'own'), split_axis=1, concat_axis=1, tile...  11.6 us
  transfers between devices with their start and end apart: 4, of which 3 were waited for; matrix products, arithmetic and copies ran while one was open for 67% of the time, Pallas kernels for 0%

commit v1 on v0

--- a/solution.py
+++ b/solution.py
@@ -1,9 +1,163 @@
+import functools
+
 import jax
 import jax.numpy as jnp
 from jax import lax
+from jax.experimental import pallas as pl
+from jax.experimental.pallas import tpu as pltpu
 from jax.sharding import PartitionSpec as P
 
 SLOTS = 2
+HI = lax.Precision.HIGHEST
+SUB = 32
+
+
+def rows_of(v, s):
+    return jnp.broadcast_to(v[s:s + 1, :], (8, 128))
+
+
+def factor_sub(wide, aug, at):
+    tiles = SUB // 8
+    wide, aug = list(wide), list(aug)
+    sub = lax.broadcasted_iota(jnp.int32, (8, 128), 0)
+    cols = {}
+    for q in range(SUB):
+        for t in range(q // 8, tiles):
+            cols[q, t] = jnp.broadcast_to(wide[t][:, at + q:at + q + 1], (8, 128))
+    diag = [None] * tiles
+    mix = [None] * tiles
+    for j in range(0, SUB, 2):
+        tj, sj = j // 8, j % 8
+        a = rows_of(cols[j, tj], sj)
+        b = rows_of(cols[j, tj], sj + 1)
+        d = rows_of(cols[j + 1, tj], sj + 1)
+        det = a * d - b * b
+        r = 1.0 / det
+        m0, m1 = {}, {}
+        for t in range(tj, tiles):
+            c0, c1 = cols[j, t], cols[j + 1, t]
+            x0 = (c0 * d - c1 * b) * r
+            x1 = (c1 * a - c0 * b) * r
+            if t == tj:
+                x0 = jnp.where(sub > sj + 1, x0, 0.0)
+                x1 = jnp.where(sub > sj + 1, x1, 0.0)
+            m0[t], m1[t] = x0, x1
+        for q in range(j + 2, SUB):
+            p0 = rows_of(cols[j, q // 8], q % 8)
+            p1 = rows_of(cols[j + 1, q // 8], q % 8)
+            for t in range(q // 8, tiles):
+                cols[q, t] = cols[q, t] - m0[t] * p0 - m1[t] * p1
+        w0, w1 = rows_of(wide[tj], sj), rows_of(wide[tj], sj + 1)
+        x0, x1 = rows_of(aug[tj], sj), rows_of(aug[tj], sj + 1)
+        for t in range(tj, tiles):
+            wide[t] = wide[t] - m0[t] * w0 - m1[t] * w1
+            aug[t] = aug[t] - m0[t] * x0 - m1[t] * x1
+        ia = 1.0 / a
+        e = det * ia
+        mu = b * ia
+        if sj == 0:
+            diag[tj] = jnp.where(sub == 0, a, e)
+            mix[tj] = jnp.where(sub == 1, mu, 0.0)
+        else:
+            diag[tj] = jnp.where(sub == sj, a, jnp.where(sub == sj + 1, e, diag[tj]))
+            mix[tj] = jnp.where(sub == sj + 1, mu, mix[tj])
+    for t in range(tiles):
+        s = lax.rsqrt(diag[t])
+        wide[t] = s * (wide[t] - mix[t] * pltpu.roll(wide[t], 1, 0))
+        aug[t] = s * (aug[t] - mix[t] * pltpu.roll(aug[t], 1, 0))
+    return wide, aug
+
+
+def dot_t(a, b, prec=HI):
+    return lax.dot_general(a, b, (((0,), (0,)), ((), ())), precision=prec, preferred_element_type=jnp.float32)
+
+
+def factor_block(diags, augs):
+    r = lax.broadcasted_iota(jnp.int32, (128, 128), 0)
+    c = lax.broadcasted_iota(jnp.int32, (128, 128), 1)
+    for x in augs:
+        x[...] = (r == c).astype(jnp.float32)
+    for i in range(128 // SUB):
+        for s, x in zip(diags, augs):
+            at = SUB * i
+            wide = [s[at + 8 * t:at + 8 * t + 8, :] for t in range(SUB // 8)]
+            aug = [x[at + 8 * t:at + 8 * t + 8, :] for t in range(SUB // 8)]
+            wide, aug = factor_sub(wide, aug, at)
+            for t in range(SUB // 8):
+                x[at + 8 * t:at + 8 * t + 8, :] = aug[t]
+            if i < 128 // SUB - 1:
+                u = jnp.concatenate(wide, axis=0)
+                rhs = jnp.concatenate([u, jnp.concatenate(aug, axis=0)], axis=1)
+                upd = dot_t(u, rhs)
+                nx = at + SUB
+                s[nx:, :] = s[nx:, :] - upd[nx:, :128]
+                x[nx:, :] = x[nx:, :] - upd[nx:, 128:]
+
+
+def refresh_kernel(n, f_ref, b_ref, fresh_ref, rot_ref, *scr):
+    m, d, x = scr[:n], scr[n:2 * n], scr[2 * n:3 * n]
+    vacant = []
+    for s in range(n):
+        pt = lax.dot_general(
+            b_ref[s], f_ref[s], (((0,), (1,)), ((), ())), preferred_element_type=jnp.float32
+        ).astype(jnp.bfloat16)
+        gram = lax.dot_general(
+            pt, pt, (((1,), (1,)), ((), ())), preferred_element_type=jnp.float32
+        )
+        r = lax.broadcasted_iota(jnp.int32, (512, 512), 0)
+        c = lax.broadcasted_iota(jnp.int32, (512, 512), 1)
+        eye = (r == c).astype(jnp.float32)
+        trace = jnp.sum(gram * eye, keepdims=True)
+        m[s][:, :512] = gram + eye * (trace == 0.0).astype(jnp.float32)
+        m[s][:, 512:] = pt.astype(jnp.float32)
+
+    def outer(k, _):
+        at = pl.multiple_of(k * 128, 128)
+        for s in range(n):
+            d[s][...] = m[s][pl.ds(at, 128), pl.ds(at, 128)]
+        factor_block(d, x)
+        for s in range(n):
+            m[s][pl.ds(at, 128), :] = jnp.dot(
+                x[s][...], m[s][pl.ds(at, 128), :], precision=HI, preferred_element_type=jnp.float32
+            )
+        for kk in range(3):
+
+            @pl.when(k == kk)
+            def _():
+                for s in range(n):
+                    lo = 128 * (kk + 1)
+                    u = m[s][lo - 128:lo, lo:512]
+                    m[s][lo:, lo:] = m[s][lo:, lo:] - dot_t(u, m[s][lo - 128:lo, lo:])
+
+        return 0
+
+    lax.fori_loop(0, 4, outer, 0)
+    for s in range(n):
+        ft = m[s][:, 512:]
+        fresh_ref[s] = ft.T.astype(jnp.bfloat16)
+        rot_ref[s] = lax.dot_general(
+            b_ref[s],
+            ft.astype(jnp.bfloat16),
+            (((0,), (1,)), ((), ())),
+            preferred_element_type=jnp.float32,
+        ).astype(jnp.bfloat16)
+
+
+def refresh(factor_slots, basis_slots, moment_slots):
+    n, order, _ = factor_slots.shape
+    out = jax.ShapeDtypeStruct((n, order, order), jnp.bfloat16)
+    fresh, rotation = pl.pallas_call(
+        functools.partial(refresh_kernel, n),
+        out_shape=(out, out),
+        scratch_shapes=[pltpu.VMEM((order, 2 * order), jnp.float32)] * n
+        + [pltpu.VMEM((128, 128), jnp.float32)] * (2 * n),
+        compiler_params=pltpu.CompilerParams(vmem_limit_bytes=40 * 2**20),
+        cost_estimate=pl.CostEstimate(flops=5 * 10**9, bytes_accessed=4 * 2**20, transcendentals=0),
+    )(factor_slots, basis_slots)
+    rotated = jnp.einsum(
+        "bcj,bjk->bck", moment_slots, rotation, preferred_element_type=jnp.float32
+    ).astype(jnp.bfloat16)
+    return (fresh, rotated)
 
 
 def pack(selector, pieces, slot_count):
@@ -20,28 +174,6 @@
         lax.all_to_all(second, ("fsdp", "own"), split_axis=1, concat_axis=1, tiled=True),
         lax.all_to_all(third, ("fsdp", "own"), split_axis=1, concat_axis=1, tiled=True),
     )
-
-
-def refresh(factor_slots, basis_slots, moment_slots):
-    block_order = factor_slots.shape[-1]
-    power = jnp.einsum(
-        "bij,bjk->bik", factor_slots, basis_slots, preferred_element_type=jnp.float32
-    ).astype(jnp.bfloat16)
-    gram_matrix = jnp.einsum("bji,bjk->bik", power, power, preferred_element_type=jnp.float32)
-    vacant = (jnp.trace(gram_matrix, axis1=1, axis2=2) == 0.0).astype(jnp.float32)
-    identity = jnp.eye(block_order, dtype=jnp.float32)
-    gram_matrix = gram_matrix + vacant[:, None, None] * identity[None]
-    lower_factor = jnp.linalg.cholesky(gram_matrix)
-    fresh_basis = lax.linalg.triangular_solve(
-        lower_factor, power.astype(jnp.float32), left_side=False, lower=True, transpose_a=True
-    ).astype(jnp.bfloat16)
-    rotation = jnp.einsum(
-        "bji,bjk->bik", basis_slots, fresh_basis, preferred_element_type=jnp.float32
-    ).astype(jnp.bfloat16)
-    rotated = jnp.einsum(
-        "bcj,bjk->bck", moment_slots, rotation, preferred_element_type=jnp.float32
-    ).astype(jnp.bfloat16)
-    return (fresh_basis, rotated)
 
 
 def per_device(factor, old_basis, moment, owner_table):

time: 463 us -> 201 us (0.43); the launches traced: 456 us -> 201 us
  other arithmetic: 256 us -> 1.58 us
  blocking collectives: 0 us -> 56.9 us
  Pallas kernels: 0 us -> 32.5 us
  matrix products: 32 us -> 3.24 us
  waiting for transfers between devices: 95.1 us -> 68.8 us
  local copies, waits for them, and re-layouts: 37 us -> 12.8 us
  starting transfers between devices: 35.2 us -> 24 us
    another operation x23 -> x0, other arithmetic: 249 us -> none  [the longest x18 164 us: refresh(): lower_factor = jnp.linalg.cholesky(gram_matrix)]
    all_to_all x0 -> x1, blocking collectives: none -> 56.9 us  [per_device(): lax.all_to_all(rotated.reshape(SLOTS, shares, col_count, block_order), ('...]
    all_to_all x1 -> x0, waiting for transfers between devices: 48.6 us -> none  [per_device(): lax.all_to_all(rotated.reshape(SLOTS, shares, col_count, block_order), ('...]
    pallas_call x0 -> x1, Pallas kernels: none -> 32.5 us  [refresh(): pl.pallas_call(functools.partial(refresh_kernel, n), out_shape=(out, out)...]
    another operation x13 -> x0, matrix products: 22.7 us -> none  [the longest x7 14.2 us: refresh(): lax.linalg.triangular_solve(lower_factor, power.astype(jnp.float32), left...]
    all_to_all x1, waiting for transfers between devices: 0.01 us -> 17.4 us  [deliver(): lax.all_to_all(third, ('fsdp', 'own'), split_axis=1, concat_axis=1, tiled...]
    another operation x17 -> x0, local copies, waits for them, and re-layouts: 16.1 us -> none
    all_to_all x1 -> x0, starting transfers between devices: 10.6 us -> none  [per_device(): lax.all_to_all(rotated.reshape(SLOTS, shares, col_count, block_order), ('...]
  transfers between devices with their start and end apart: 4 -> 3, of which waited for: 3 -> 3; matrix products, arithmetic and copies ran while one was open for 67% -> 3% of each run, Pallas kernels for 0% -> 16%
where the time goes in v1:
time: 201 us
  waiting for transfers between devices  68.8 us (34%)
  blocking collectives  56.9 us (28%)
  Pallas kernels  32.5 us (16%)
  starting transfers between devices  24 us (12%)
  local copies, waits for them, and re-layouts  12.8 us (6%)
  matrix products  3.24 us (2%)
    all_to_all x1, blocking collectives, per_device(): lax.all_to_all(rotated.reshape(SLOTS, shares, col_count, block_order), ('...  56.9 us
    pallas_call x1, Pallas kernels, refresh(): pl.pallas_call(functools.partial(refresh_kernel, n), out_shape=(out, out)...  32.5 us
    all_to_all x1, waiting for transfers between devices, deliver(): lax.all_to_all(first, ('fsdp', 'own'), split_axis=1, concat_axis=1, tiled...  26.4 us
    all_to_all x1, waiting for transfers between devices, deliver(): lax.all_to_all(second, ('fsdp', 'own'), split_axis=1, concat_axis=1, tile...  24.9 us
    all_to_all x1, waiting for transfers between devices, deliver(): lax.all_to_all(third, ('fsdp', 'own'), split_axis=1, concat_axis=1, tiled...  17.4 us
    all_to_all x1, starting transfers between devices, deliver(): lax.all_to_all(first, ('fsdp', 'own'), split_axis=1, concat_axis=1, tiled...  11.6 us
    unnamed x16, local copies, waits for them, and re-layouts  8.21 us
    all_to_all x1, starting transfers between devices, deliver(): lax.all_to_all(third, ('fsdp', 'own'), split_axis=1, concat_axis=1, tiled...  6.2 us
  transfers between devices with their start and end apart: 3, of which 3 were waited for; matrix products, arithmetic and copies ran while one was open for 3% of the time, Pallas kernels for 16%

profile of v1, /device:TPU:1, one launch (start us, length us, event | category | flops | bytes accessed | tf_op | source)
XLA Modules:
  0.0 200.5 jit_solution(6914391382691765599)
XLA Ops:
  0.6 0.9 convert_reduce_fusion
  1.5 0.7 multiply_add_fusion
  2.2 1.2 copy.31
  3.4 0.4 convolution_convert_fusion.3
  4.2 1.1 copy.23
  5.3 11.6 %all-to-all-start.1 = ((bf16[2,64,8,512]{3,2,0,1:T(8,128)(2,1)}), bf16[2,64,8,512]{3,2,0,1:T(8,128)(2,1)S(1)}, u32[]{:S(2)}, u32[]{:S(2)}) async-start(bf16[2,64,8,512]{3,2,0,1:T(8,128)(2,1)} %copy.23), calls=%async_computation.1 | async-start | bytes 2097152 | tf_op jit(solution)/shard_map/all_to_all | solution.py:173
  18.0 1.1 copy.25
  19.1 26.4 %all-to-all-done.1 = bf16[2,64,8,512]{3,2,0,1:T(8,128)(2,1)S(1)} async-done(((bf16[2,64,8,512]{3,2,0,1:T(8,128)(2,1)}), bf16[2,64,8,512]{3,2,0,1:T(8,128)(2,1)S(1)}, u32[]{:S(2)}, u32[]{:S(2)}) %all-to-all-start.1) | async-done | bytes 1048608 | tf_op jit(solution)/shard_map/all_to_all | solution.py:173
  45.5 6.2 %all-to-all-start.2 = ((bf16[2,64,8,512]{3,2,0,1:T(8,128)(2,1)}), bf16[2,64,8,512]{3,2,0,1:T(8,128)(2,1)S(1)}, u32[]{:S(2)}, u32[]{:S(2)}) async-start(bf16[2,64,8,512]{3,2,0,1:T(8,128)(2,1)} %copy.25), calls=%async_computation.2 | async-start | bytes 2097152 | tf_op jit(solution)/shard_map/all_to_all | solution.py:174
  51.7 0.5 copy.29
  52.3 0.7 convolution_convert_fusion
  53.0 0.8 copy.30
  53.8 1.5 copy.21
  55.4 24.9 %all-to-all-done.2 = bf16[2,64,8,512]{3,2,0,1:T(8,128)(2,1)S(1)} async-done(((bf16[2,64,8,512]{3,2,0,1:T(8,128)(2,1)}), bf16[2,64,8,512]{3,2,0,1:T(8,128)(2,1)S(1)}, u32[]{:S(2)}, u32[]{:S(2)}) %all-to-all-start.2) | async-done | bytes 1048608 | tf_op jit(solution)/shard_map/all_to_all | solution.py:174
  80.3 1.0 copy-done
  81.3 6.2 %all-to-all-start = ((bf16[2,64,16,512]{3,2,0,1:T(8,128)(2,1)}), bf16[2,64,16,512]{3,2,0,1:T(8,128)(2,1)S(1)}, u32[]{:S(2)}, u32[]{:S(2)}) async-start(bf16[2,64,16,512]{3,2,0,1:T(8,128)(2,1)} %copy.21), calls=%async_computation | async-start | bytes 4194304 | tf_op jit(solution)/shard_map/all_to_all | solution.py:175
  87.6 1.1 copy-done.1
  88.8 32.5 %shard_map.59 = (bf16[2,512,512]{2,1,0:T(8,128)(2,1)}, bf16[2,512,512]{2,1,0:T(8,128)(2,1)S(1)}) custom-call(bf16[2,512,512]{2,1,0:T(8,128)(2,1)S(1)} %bitcast.37, bf16[2,512,512]{2,1,0:T(8,128)(2,1)S(1)} %bitcast.38), custom_call_target="tpu_custom_call" | custom-call | flops 5000000000 | bytes 4194304 | tf_op jit(solution)/shard_map/pallas_call | solution.py:149
  121.3 17.4 %all-to-all-done = bf16[2,64,16,512]{3,2,0,1:T(8,128)(2,1)S(1)} async-done(((bf16[2,64,16,512]{3,2,0,1:T(8,128)(2,1)}), bf16[2,64,16,512]{3,2,0,1:T(8,128)(2,1)S(1)}, u32[]{:S(2)}, u32[]{:S(2)}) %all-to-all-start) | async-done | bytes 2097184 | tf_op jit(solution)/shard_map/all_to_all | solution.py:175
  138.9 1.2 convolution_convert_fusion.4
  140.4 56.9 %all_to_all.20 = bf16[2,64,16,512]{3,2,0,1:T(8,128)(2,1)S(1)} all-to-all(bf16[2,64,16,512]{3,2,0,1:T(8,128)(2,1)S(1)} %copy.27), channel_id=1, replica_groups=mesh['fsdp'=32,'layer'=8,'own'=2] {'fsdp','own'}, dimensions={1} | all-to-all | bytes 4194304 | tf_op jit(solution)/shard_map/all_to_all | solution.py:199
  197.5 1.4 copy.35
  198.8 0.5 convolution_convert_fusion.1
  199.3 1.2 copy.36
  (15 shorter events, 2.1 us)
Async XLA Ops:
  4.2 12.8 %copy-start.3 = (bf16[56,8,512]{2,1,0:T(8,128)(2,1)S(1)}, bf16[56,8,512]{2,1,0:T(8,128)(2,1)}, u32[]{:S(2)}) copy-start(bf16[56,8,512]{2,1,0:T(8,128)(2,1)} %param.5) | copy-start | bytes 1376260
  5.3 40.2 %all-to-all-start.1 = ((bf16[2,64,8,512]{3,2,0,1:T(8,128)(2,1)}), bf16[2,64,8,512]{3,2,0,1:T(8,128)(2,1)S(1)}, u32[]{:S(2)}, u32[]{:S(2)}) async-start(bf16[2,64,8,512]{3,2,0,1:T(8,128)(2,1)} %copy.23), calls=%async_computation.1 | async-start | bytes 2097152 | tf_op jit(solution)/shard_map/all_to_all | solution.py:173
  18.0 33.8 %copy-start.2 = (bf16[56,16,512]{2,1,0:T(8,128)(2,1)S(1)}, bf16[56,16,512]{2,1,0:T(8,128)(2,1)}, u32[]{:S(2)}) copy-start(bf16[56,16,512]{2,1,0:T(8,128)(2,1)} %param.6) | copy-start | bytes 2752516
  45.5 34.8 %all-to-all-start.2 = ((bf16[2,64,8,512]{3,2,0,1:T(8,128)(2,1)}), bf16[2,64,8,512]{3,2,0,1:T(8,128)(2,1)S(1)}, u32[]{:S(2)}, u32[]{:S(2)}) async-start(bf16[2,64,8,512]{3,2,0,1:T(8,128)(2,1)} %copy.25), calls=%async_computation.2 | async-start | bytes 2097152 | tf_op jit(solution)/shard_map/all_to_all | solution.py:174
  80.3 1.0 copy-start
  81.3 57.4 %all-to-all-start = ((bf16[2,64,16,512]{3,2,0,1:T(8,128)(2,1)}), bf16[2,64,16,512]{3,2,0,1:T(8,128)(2,1)S(1)}, u32[]{:S(2)}, u32[]{:S(2)}) async-start(bf16[2,64,16,512]{3,2,0,1:T(8,128)(2,1)} %copy.21), calls=%async_computation | async-start | bytes 4194304 | tf_op jit(solution)/shard_map/all_to_all | solution.py:175
  87.5 1.2 copy-start.1

commit v2 on v1

v2 whole, which is shorter than its diff:
```python
import functools

import jax
import jax.numpy as jnp
from jax import lax
from jax.experimental import pallas as pl
from jax.experimental.pallas import tpu as pltpu
from jax.sharding import PartitionSpec as P

SLOTS = 2
SHARES = 64
BLOCKS = 56
MOVERS = 56
ORDER = 512
PANEL = 128
FULL = ORDER + 3 * PANEL
SHORT = ORDER + 2 * PANEL
HI = lax.Precision.HIGHEST
SUB = 32


def rows_of(v, s):
    return jnp.broadcast_to(v[s:s + 1, :], (8, 128))


def factor_sub(wide, aug, at):
    tiles = SUB // 8
    wide, aug = list(wide), list(aug)
    sub = lax.broadcasted_iota(jnp.int32, (8, 128), 0)
    cols = {}
    for q in range(SUB):
        for t in range(q // 8, tiles):
            cols[q, t] = jnp.broadcast_to(wide[t][:, at + q:at + q + 1], (8, 128))
    diag = [None] * tiles
    mix = [None] * tiles
    for j in range(0, SUB, 2):
        tj, sj = j // 8, j % 8
        a = rows_of(cols[j, tj], sj)
        b = rows_of(cols[j, tj], sj + 1)
        d = rows_of(cols[j + 1, tj], sj + 1)
        det = a * d - b * b
        r = 1.0 / det
        m0, m1 = {}, {}
        for t in range(tj, tiles):
            c0, c1 = cols[j, t], cols[j + 1, t]
            x0 = (c0 * d - c1 * b) * r
            x1 = (c1 * a - c0 * b) * r
            if t == tj:
                x0 = jnp.where(sub > sj + 1, x0, 0.0)
                x1 = jnp.where(sub > sj + 1, x1, 0.0)
            m0[t], m1[t] = x0, x1
        for q in range(j + 2, SUB):
            p0 = rows_of(cols[j, q // 8], q % 8)
            p1 = rows_of(cols[j + 1, q // 8], q % 8)
            for t in range(q // 8, tiles):
                cols[q, t] = cols[q, t] - m0[t] * p0 - m1[t] * p1
        w0, w1 = rows_of(wide[tj], sj), rows_of(wide[tj], sj + 1)
        x0, x1 = rows_of(aug[tj], sj), rows_of(aug[tj], sj + 1)
        for t in range(tj, tiles):
            wide[t] = wide[t] - m0[t] * w0 - m1[t] * w1
            aug[t] = aug[t] - m0[t] * x0 - m1[t] * x1
        ia = 1.0 / a
        e = det * ia
        mu = b * ia
        if sj == 0:
            diag[tj] = jnp.where(sub == 0, a, e)
            mix[tj] = jnp.where(sub == 1, mu, 0.0)
        else:
            diag[tj] = jnp.where(sub == sj, a, jnp.where(sub == sj + 1, e, diag[tj]))
            mix[tj] = jnp.where(sub == sj + 1, mu, mix[tj])
    for t in range(tiles):
        s = lax.rsqrt(diag[t])
        wide[t] = s * (wide[t] - mix[t] * pltpu.roll(wide[t], 1, 0))
        aug[t] = s * (aug[t] - mix[t] * pltpu.roll(aug[t], 1, 0))
    return wide, aug


def dot_t(a, b, prec=HI):
    return lax.dot_general(a, b, (((0,), (0,)), ((), ())), precision=prec, preferred_element_type=jnp.float32)


def factor_block(diags, augs):
    r = lax.broadcasted_iota(jnp.int32, (128, 128), 0)
    c = lax.broadcasted_iota(jnp.int32, (128, 128), 1)
    for x in augs:
        x[...] = (r == c).astype(jnp.float32)
    for i in range(128 // SUB):
        for s, x in zip(diags, augs):
            at = SUB * i
            wide = [s[at + 8 * t:at + 8 * t + 8, :] for t in range(SUB // 8)]
            aug = [x[at + 8 * t:at + 8 * t + 8, :] for t in range(SUB // 8)]
            wide, aug = factor_sub(wide, aug, at)
            for t in range(SUB // 8):
                x[at + 8 * t:at + 8 * t + 8, :] = aug[t]
            if i < 128 // SUB - 1:
                u = jnp.concatenate(wide, axis=0)
                rhs = jnp.concatenate([u, jnp.concatenate(aug, axis=0)], axis=1)
                upd = dot_t(u, rhs)
                nx = at + SUB
                s[nx:, :] = s[nx:, :] - upd[nx:, :128]
                x[nx:, :] = x[nx:, :] - upd[nx:, 128:]


def at_share(t):
    return {"fsdp": t // 2, "own": lax.rem(t, 2)}


def remote(src, dst, send, recv, t):
    return pltpu.make_async_remote_copy(
        src_ref=src,
        dst_ref=dst,
        send_sem=send,
        recv_sem=recv,
        device_id=at_share(t),
        device_id_type=pl.DeviceIdType.MESH,
    )


def mover(d):
    return jnp.where(d < 48, d, 2 * d - 48)


def wide_f32(x):
    return x.astype(jnp.float32).reshape(-1, x.shape[-1])


def refresh_kernel(
    table,
    factor,
    basis,
    moment,
    moment_out,
    owner_basis,
    send0,
    send1,
    sendm,
    got0,
    got1,
    gotm,
    backs,
    backr,
    old,
    work,
    diag,
    inverse,
    rotation,
    sems,
    recv0,
    recv1,
    recvm,
    recvb,
):
    me = lax.axis_index("fsdp") * 2 + lax.axis_index("own")
    panel = me // 16
    long = panel < 2
    idle = (me >= 48) & (lax.rem(me, 2) == 1)
    moves = jnp.logical_not(idle)
    peer = lax.rem(me + 1, SHARES)

    barrier = pltpu.get_barrier_semaphore()

    def greet(k, _):
        pl.semaphore_signal(
            barrier,
            inc=1,
            device_id=at_share(lax.rem(me + k, SHARES)),
            device_id_type=pl.DeviceIdType.MESH,
        )
        return 0

    lax.fori_loop(1, SHARES, greet, 0)

    def pack(slot, send, t):
        b = table[slot * SHARES + t]
        send[t, :, :ORDER] = basis[b]
        for q in range(3):
            lane = pl.multiple_of(lax.rem(panel + q, 4) * PANEL, PANEL)
            send[t, :, ORDER + q * PANEL:ORDER + (q + 1) * PANEL] = factor[b, :, pl.ds(lane, PANEL)]

    def post(slot, send, got, recv, t):
        @pl.when(long)
        def _():
            remote(send.at[t], got.at[me], sems.at[slot], recv.at[0], t).start()

        @pl.when(jnp.logical_not(long))
        def _():
            remote(
                send.at[t, :, :SHORT], got.at[me, :, :SHORT], sems.at[slot], recv.at[1], t
            ).start()

    def arrive(got, recv):
        @pl.when(long)
        def _():
            remote(got.at[0:31], got.at[0:31], recv.at[0], recv.at[0], peer).wait_recv()
            part = got.at[0:32, :, :SHORT]
            remote(part, part, recv.at[1], recv.at[1], peer).wait_recv()

        @pl.when(jnp.logical_not(long))
        def _():
            remote(got.at[0:32], got.at[0:32], recv.at[0], recv.at[0], peer).wait_recv()
            part = got.at[0:31, :, :SHORT]
            remote(part, part, recv.at[1], recv.at[1], peer).wait_recv()

    def sent(slot, send):
        @pl.when(long)
        def _():
            remote(send.at[0:63], send.at[0:63], sems.at[slot], recv0.at[0], peer).wait_send()

        @pl.when(jnp.logical_not(long))
        def _():
            part = send.at[0:63, :, :SHORT]
            remote(part, part, sems.at[slot], recv0.at[0], peer).wait_send()

    def pack0(t, _):
        pack(0, send0, t)
        return 0

    lax.fori_loop(0, SHARES, pack0, 0)
    got0[me] = send0[me]
    pl.semaphore_wait(barrier, SHARES - 1)

    def post0(k, _):
        post(0, send0, got0, recv0, lax.rem(me + k, SHARES))
        return 0

    lax.fori_loop(1, SHARES, post0, 0)

    def pack1(t, _):
        pack(1, send1, t)
        sendm[t] = moment[table[t]]
        return 0

    lax.fori_loop(0, SHARES, pack1, 0)
    got1[me] = send1[me]
    gotm[me] = sendm[me]

    def load(got):
        whole = wide_f32(got[:, :, :ORDER]).astype(jnp.bfloat16)
        old[...] = whole
        part = {}
        for p in range(4):
            for q in range(3 if p < 2 else 2):
                lo = ORDER + q * PANEL
                x = wide_f32(got[16 * p:16 * p + 16, :, lo:lo + PANEL])
                part[p, (p + q) % 4] = x
                if q:
                    part[(p + q) % 4, p] = x.T
        full = jnp.concatenate(
            [jnp.concatenate([part[p, q] for q in range(4)], axis=1) for p in range(4)], axis=0
        ).astype(jnp.bfloat16)
        pt = lax.dot_general(
            whole, full, (((0,), (0,)), ((), ())), preferred_element_type=jnp.float32
        ).astype(jnp.bfloat16)
        work[:, :ORDER] = lax.dot_general(
            pt, pt, (((1,), (1,)), ((), ())), preferred_element_type=jnp.float32
        )
        work[:, ORDER:] = pt.astype(jnp.float32)

    def panel_step(k):
        at = pl.multiple_of(k * PANEL, PANEL)
        diag[...] = work[pl.ds(at, PANEL), pl.ds(at, PANEL)]
        factor_block([diag], [inverse])
        work[pl.ds(at, PANEL), :] = jnp.dot(
            inverse[...], work[pl.ds(at, PANEL), :], precision=HI, preferred_element_type=jnp.float32
        )
        for kk in range(3):

            @pl.when(k == kk)
            def _():
                lo = PANEL * (kk + 1)
                u = work[lo - PANEL:lo, lo:ORDER]
                work[lo:, lo:] = work[lo:, lo:] - dot_t(u, work[lo - PANEL:lo, lo:])

    def keep(slot):
        there = jnp.full((ORDER, ORDER), table[3 * SHARES + slot], jnp.int32)
        owner_basis[0, slot] = jnp.where(there > 0, work[:, ORDER:].T, 0.0).astype(jnp.bfloat16)

    def post1(k, _):
        post(1, send1, got1, recv1, lax.rem(me + k, SHARES))
        return 0

    def postm(k, _):
        t = mover(lax.rem(me + k, MOVERS))

        @pl.when(t != me)
        def _():
            remote(sendm.at[t], gotm.at[me], sems.at[2], recvm, t).start()

        return 0

    def rotate(i, _):
        cut = lax.rem(me // 8 + i, 8)
        rows = pl.ds(cut * 8, 8)
        x = gotm[rows].reshape(8 * 16, ORDER)
        y = jnp.dot(x, rotation[...], preferred_element_type=jnp.float32).astype(jnp.bfloat16)
        backs[rows] = y.reshape(8, 16, ORDER)

        def postb(k, _):
            t = cut * 8 + k

            @pl.when(t != me)
            def _():
                remote(backs.at[t], backr.at[me], sems.at[3], recvb, t).start()

            return 0

        lax.fori_loop(0, 8, postb, 0)
        return 0

    def step(i, _):
        @pl.when(i == 0)
        def _():
            arrive(got0, recv0)
            lax.fori_loop(1, SHARES, post1, 0)
            load(got0)

        @pl.when(i == 2)
        def _():
            lax.fori_loop(0, MOVERS, postm, 0)

        @pl.when(i == 4)
        def _():
            keep(0)
            rotation[...] = lax.dot_general(
                old[...],
                work[:, ORDER:].astype(jnp.bfloat16),
                (((0,), (1,)), ((), ())),
                preferred_element_type=jnp.float32,
            ).astype(jnp.bfloat16)
            arrive(got1, recv1)
            load(got1)

        @pl.when((i == 6) & moves)
        def _():
            remote(gotm.at[0:63], gotm.at[0:63], recvm, recvm, peer).wait_recv()
            lax.fori_loop(0, 8, rotate, 0)
            backr[me] = backs[me]

        panel_step(lax.rem(i, 4))
        return 0

    lax.fori_loop(0, 8, step, 0)
    keep(1)

    @pl.when(moves)
    def _():
        remote(backr.at[0:55], backr.at[0:55], recvb, recvb, peer).wait_recv()

    @pl.when(idle)
    def _():
        remote(backr.at[0:56], backr.at[0:56], recvb, recvb, peer).wait_recv()

    def place(b, _):
        moment_out[b] = backr[table[2 * SHARES + b]]
        return 0

    lax.fori_loop(0, BLOCKS, place, 0)

    sent(0, send0)
    sent(1, send1)

    @pl.when(moves)
    def _():
        remote(sendm.at[0:55], sendm.at[0:55], sems.at[2], recvm, peer).wait_send()
        remote(backs.at[0:63], backs.at[0:63], sems.at[3], recvb, peer).wait_send()

    @pl.when(idle)
    def _():
        remote(sendm.at[0:56], sendm.at[0:56], sems.at[2], recvm, peer).wait_send()


def plan(owners, me):
    blocks = jnp.arange(BLOCKS, dtype=jnp.int32)
    shares = jnp.arange(SHARES, dtype=jnp.int32)
    same = (owners[:, None] == owners[None, :]) & (blocks[None, :] < blocks[:, None])
    rank = jnp.sum(same.astype(jnp.int32), axis=1)
    idle = (shares >= 48) & (shares % 2 == 1)
    mine = owners[None, :] == shares[:, None]
    first = mine & (rank == 0)[None, :]
    second = mine & (rank == 1)[None, :]
    vacant = jnp.logical_not(jnp.any(mine, axis=1) | idle)
    guest = (rank == 1) | ((owners >= 48) & (owners % 2 == 1))
    vacant_at = jnp.sum(vacant[None, :] & (shares[None, :] < shares[:, None]), axis=1)
    guest_at = jnp.sum(guest[None, :] & (blocks[None, :] < blocks[:, None]), axis=1)
    hosted = vacant[:, None] & guest[None, :] & (vacant_at[:, None] == guest_at[None, :])
    slot0 = jnp.sum(jnp.where(first | hosted, blocks[None, :], 0), axis=1)
    slot1 = jnp.sum(jnp.where(second, blocks[None, :], 0), axis=1)
    moved = hosted | (first & jnp.logical_not(idle)[:, None])
    where = jnp.sum(jnp.where(moved, shares[:, None], 0), axis=0)
    keeps = jnp.stack([jnp.any(owners == me), jnp.any((owners == me) & (rank == 1))])
    return jnp.concatenate(
        [slot0, slot1, jnp.pad(where, (0, SHARES - BLOCKS)), jnp.pad(keeps.astype(jnp.int32), (0, SHARES - 2))]
    ).astype(jnp.int32)


def per_device(factor, old_basis, moment, owner_table):
    me = lax.axis_index("fsdp") * 2 + lax.axis_index("own")
    table = plan(owner_table[:, 0], me)
    bf16 = jnp.bfloat16
    vmem = pl.BlockSpec(memory_space=pltpu.VMEM)
    return pl.pallas_call(
        refresh_kernel,
        out_shape=(
            jax.ShapeDtypeStruct(moment.shape, bf16),
            jax.ShapeDtypeStruct((1, SLOTS, ORDER, ORDER), bf16),
        ),
        in_specs=[pl.BlockSpec(memory_space=pltpu.SMEM), vmem, vmem, vmem],
        out_specs=(vmem, vmem),
        scratch_shapes=[
            pltpu.VMEM((SHARES, 8, FULL), bf16),
            pltpu.VMEM((SHARES, 8, FULL), bf16),
            pltpu.VMEM((SHARES, 16, ORDER), bf16),
            pltpu.VMEM((SHARES, 8, FULL), bf16),
            pltpu.VMEM((SHARES, 8, FULL), bf16),
            pltpu.VMEM((SHARES, 16, ORDER), bf16),
            pltpu.VMEM((SHARES, 16, ORDER), bf16),
            pltpu.VMEM((SHARES, 16, ORDER), bf16),
            pltpu.VMEM((ORDER, ORDER), bf16),
            pltpu.VMEM((ORDER, 2 * ORDER), jnp.float32),
            pltpu.VMEM((PANEL, PANEL), jnp.float32),
            pltpu.VMEM((PANEL, PANEL), jnp.float32),
            pltpu.VMEM((ORDER, ORDER), bf16),
            pltpu.SemaphoreType.DMA((4,)),
            pltpu.SemaphoreType.DMA((2,)),
            pltpu.SemaphoreType.DMA((2,)),
            pltpu.SemaphoreType.DMA,
            pltpu.SemaphoreType.DMA,
        ],
        compiler_params=pltpu.CompilerParams(
            collective_id=0, has_side_effects=True, vmem_limit_bytes=48 * 2**20
        ),
        cost_estimate=pl.CostEstimate(flops=8 * 10**9, bytes_accessed=4 * 2**20, transcendentals=0),
    )(table, factor, old_basis, moment)


def solution(mesh):
    in_specs = (
        P("layer", ("fsdp", "own"), None),
        P("layer", ("fsdp", "own"), None),
        P("layer", ("fsdp", "own"), None),
        P("layer", None),
    )
    out_specs = (P("layer", ("fsdp", "own"), None), P("layer", ("fsdp", "own"), None, None))
    return jax.shard_map(
        per_device, mesh=mesh, in_specs=in_specs, out_specs=out_specs, check_vma=False
    )
```

time: 201 us -> 113 us (0.56)
  Pallas kernels: 32.5 us -> 104 us
  waiting for transfers between devices: 68.8 us -> 0 us
  blocking collectives: 56.9 us -> 0 us
  starting transfers between devices: 24 us -> 0 us
  local copies, waits for them, and re-layouts: 12.8 us -> 5.76 us
  matrix products: 3.24 us -> 0 us
    pallas_call x1, Pallas kernels: 32.5 us -> 104 us  [per_device(): pl.pallas_call(refresh_kernel, out_shape=(jax.ShapeDtypeStruct(moment.sha...]
    all_to_all x3 -> x0, waiting for transfers between devices: 68.8 us -> none  [the longest x1 26.4 us: deliver(): lax.all_to_all(first, ('fsdp', 'own'), split_axis=1, concat_axis=1, tiled...]
    all_to_all x1 -> x0, blocking collectives: 56.9 us -> none  [per_device(): lax.all_to_all(rotated.reshape(SLOTS, shares, col_count, block_order), ('...]
    all_to_all x3 -> x0, starting transfers between devices: 24 us -> none  [the longest x1 11.6 us: deliver(): lax.all_to_all(first, ('fsdp', 'own'), split_axis=1, concat_axis=1, tiled...]
    reshape x4 -> x0, local copies, waits for them, and re-layouts: 4.05 us -> none  [the longest x3 3.81 us: pack(): flat.reshape(slot_count, share_count, pieces.shape[1], pieces.shape[2])]
    dot_general x5 -> x0, matrix products: 3.24 us -> none  [the longest x3 1.52 us: pack(): jnp.dot(selector, pieces.reshape(pieces.shape[0], -1), preferred_element_...]
    unnamed x16 -> x10, local copies, waits for them, and re-layouts: 8.21 us -> 5.76 us
  transfers between devices with their start and end apart: 3 -> 0, of which waited for: 3 -> 0; matrix products, arithmetic and copies ran while one was open for 3% -> 0% of each run, Pallas kernels for 16% -> 0%
where the time goes in v2:
time: 113 us
  Pallas kernels  104 us (92%)
  local copies, waits for them, and re-layouts  5.76 us (5%)
  other arithmetic  2.82 us (2%)
    pallas_call x1, Pallas kernels, per_device(): pl.pallas_call(refresh_kernel, out_shape=(jax.ShapeDtypeStruct(moment.sha...  104 us
    unnamed x10, local copies, waits for them, and re-layouts  5.76 us

profile of v2, /device:TPU:1, one launch (start us, length us, event | category | flops | bytes accessed | tf_op | source)
XLA Modules:
  0.0 112.8 jit_solution(5449922089569663732)
XLA Ops:
  0.6 0.0 copy-start.3
  0.6 0.6 copy-done.3
  1.3 0.2 convert_reduce_fusion.2
  1.5 0.1 fusion.4
  1.6 0.1 convert_reduce_fusion
  1.7 0.6 compare_reduce_fusion
  2.3 0.1 convert_reduce_fusion.1
  2.5 0.2 select_reduce_fusion.2
  2.7 1.4 %pad_add_fusion = pred[2]{0:T(512)(128)(4,1)S(1)} fusion(pred[1]{0:T(512)(128)(4,1)} %bitcast.2, pred[1]{0:T(512)(128)(4,1)} %bitcast.1), kind=kLoop, calls=%fused_computation.21 | loop fusion | flops 2 | bytes 4 | tf_op jit(solution)/shard_map/stack | solution.py:390
  4.0 0.1 fusion.9.table
  4.1 0.0 copy-start
  4.1 1.2 %copy-done = bf16[56,16,512]{2,1,0:T(8,128)(2,1)S(1)} copy-done((bf16[56,16,512]{2,1,0:T(8,128)(2,1)S(1)}, bf16[56,16,512]{2,1,0:T(8,128)(2,1)}, u32[]{:S(2)}) %copy-start) | copy-done | bytes 917528
  5.3 0.0 copy-start.1
  5.3 1.0 copy-done.1
  6.3 0.0 copy-start.2
  6.3 1.0 copy-done.2
  7.3 103.6 %shard_map.59 = (bf16[56,16,512]{2,1,0:T(8,128)(2,1)S(1)}, bf16[1,2,512,512]{3,2,1,0:T(8,128)(2,1)S(1)}) custom-call(s32[256]{0:T(256)S(1)} %fusion.9.table, bf16[56,8,512]{2,1,0:T(8,128)(2,1)S(1)} %copy-done.1, bf16[56,8,512]{2,1,0:T(8,128)(2,1)S(1)} %copy-done.2, bf16[56,16,512]{2,1,0:T(8,128)(2,1)S(1)} %copy-done), custom_call_target="tpu_custom_call" | custom-call | flops 8000000000 | bytes 4194304 | tf_op jit(solution)/shard_map/pallas_call | solution.py:401
  110.9 0.9 copy.8
  111.9 1.0 copy.9
  (2 shorter events, 0.0 us)
Async XLA Ops:
  0.6 0.7 copy-start.3
  4.1 1.2 %copy-start = (bf16[56,16,512]{2,1,0:T(8,128)(2,1)S(1)}, bf16[56,16,512]{2,1,0:T(8,128)(2,1)}, u32[]{:S(2)}) copy-start(bf16[56,16,512]{2,1,0:T(8,128)(2,1)} %moment.1) | copy-start | bytes 2752516
  5.3 1.0 copy-start.1
  6.3 1.0 copy-start.2

commit v3 on v2

--- a/solution.py
+++ b/solution.py
@@ -10,7 +10,6 @@
 SLOTS = 2
 SHARES = 64
 BLOCKS = 56
-MOVERS = 56
 ORDER = 512
 PANEL = 128
 FULL = ORDER + 3 * PANEL
@@ -116,8 +115,8 @@
     )
 
 
-def mover(d):
-    return jnp.where(d < 48, d, 2 * d - 48)
+def is_idle(t):
+    return (lax.rem(t, 2) == 1) & (lax.rem(t // 2, 4) == t // 16)
 
 
 def wide_f32(x):
@@ -125,10 +124,10 @@
 
 
 def refresh_kernel(
-    table,
-    factor,
-    basis,
-    moment,
+    owners,
+    factor_hbm,
+    basis_hbm,
+    moment_hbm,
     moment_out,
     owner_basis,
     send0,
@@ -144,16 +143,30 @@
     diag,
     inverse,
     rotation,
+    factor,
+    basis,
+    moment,
+    planned,
+    table,
     sems,
     recv0,
     recv1,
     recvm,
     recvb,
+    local,
 ):
+    fetches = [
+        pltpu.make_async_copy(src, dst, local.at[i])
+        for i, (src, dst) in enumerate(
+            ((basis_hbm, basis), (factor_hbm, factor), (moment_hbm, moment))
+        )
+    ]
+    for fetch in fetches:
+        fetch.start()
     me = lax.axis_index("fsdp") * 2 + lax.axis_index("own")
     panel = me // 16
     long = panel < 2
-    idle = (me >= 48) & (lax.rem(me, 2) == 1)
+    idle = is_idle(me)
     moves = jnp.logical_not(idle)
     peer = lax.rem(me + 1, SHARES)
 
@@ -170,8 +183,15 @@
 
     lax.fori_loop(1, SHARES, greet, 0)
 
+    plan(owners, planned)
+    tables = pltpu.make_async_copy(planned, table, local.at[3])
+    tables.start()
+    for fetch in fetches[:2]:
+        fetch.wait()
+    tables.wait()
+
     def pack(slot, send, t):
-        b = table[slot * SHARES + t]
+        b = table[slot, t]
         send[t, :, :ORDER] = basis[b]
         for q in range(3):
             lane = pl.multiple_of(lax.rem(panel + q, 4) * PANEL, PANEL)
@@ -225,14 +245,35 @@
 
     lax.fori_loop(1, SHARES, post0, 0)
 
+    fetches[2].wait()
+
+    def packm(t, _):
+        sendm[t] = moment[table[0, t]]
+        return 0
+
+    lax.fori_loop(0, SHARES, packm, 0)
+    gotm[me] = sendm[me]
+
+    def postm(half):
+        def body(k, _):
+            t = lax.rem(16 * panel + 32 * half + lax.rem(lax.rem(me, 16) + k, 32), SHARES)
+
+            @pl.when((t != me) & jnp.logical_not(is_idle(t)))
+            def _():
+                remote(sendm.at[t], gotm.at[me], sems.at[2], recvm.at[half], t).start()
+
+            return 0
+
+        lax.fori_loop(0, 32, body, 0)
+
+    postm(0)
+
     def pack1(t, _):
         pack(1, send1, t)
-        sendm[t] = moment[table[t]]
         return 0
 
     lax.fori_loop(0, SHARES, pack1, 0)
     got1[me] = send1[me]
-    gotm[me] = sendm[me]
 
     def load(got):
         whole = wide_f32(got[:, :, :ORDER]).astype(jnp.bfloat16)
@@ -272,24 +313,15 @@
                 work[lo:, lo:] = work[lo:, lo:] - dot_t(u, work[lo - PANEL:lo, lo:])
 
     def keep(slot):
-        there = jnp.full((ORDER, ORDER), table[3 * SHARES + slot], jnp.int32)
+        there = jnp.full((ORDER, ORDER), table[3 + slot, me], jnp.int32)
         owner_basis[0, slot] = jnp.where(there > 0, work[:, ORDER:].T, 0.0).astype(jnp.bfloat16)
 
     def post1(k, _):
         post(1, send1, got1, recv1, lax.rem(me + k, SHARES))
         return 0
 
-    def postm(k, _):
-        t = mover(lax.rem(me + k, MOVERS))
-
-        @pl.when(t != me)
-        def _():
-            remote(sendm.at[t], gotm.at[me], sems.at[2], recvm, t).start()
-
-        return 0
-
     def rotate(i, _):
-        cut = lax.rem(me // 8 + i, 8)
+        cut = lax.rem(2 * panel + 6 + i, 8)
         rows = pl.ds(cut * 8, 8)
         x = gotm[rows].reshape(8 * 16, ORDER)
         y = jnp.dot(x, rotation[...], preferred_element_type=jnp.float32).astype(jnp.bfloat16)
@@ -316,7 +348,7 @@
 
         @pl.when(i == 2)
         def _():
-            lax.fori_loop(0, MOVERS, postm, 0)
+            postm(1)
 
         @pl.when(i == 4)
         def _():
@@ -327,14 +359,20 @@
                 (((0,), (1,)), ((), ())),
                 preferred_element_type=jnp.float32,
             ).astype(jnp.bfloat16)
+
+            @pl.when(moves)
+            def _():
+                remote(gotm.at[0:31], gotm.at[0:31], sems.at[2], recvm.at[0], peer).wait_recv()
+                lax.fori_loop(0, 4, rotate, 0)
+                backr[me] = backs[me]
+
             arrive(got1, recv1)
             load(got1)
 
         @pl.when((i == 6) & moves)
         def _():
-            remote(gotm.at[0:63], gotm.at[0:63], recvm, recvm, peer).wait_recv()
-            lax.fori_loop(0, 8, rotate, 0)
-            backr[me] = backs[me]
+            remote(gotm.at[0:32], gotm.at[0:32], sems.at[2], recvm.at[1], peer).wait_recv()
+            lax.fori_loop(4, 8, rotate, 0)
 
         panel_step(lax.rem(i, 4))
         return 0
@@ -351,7 +389,7 @@
         remote(backr.at[0:56], backr.at[0:56], recvb, recvb, peer).wait_recv()
 
     def place(b, _):
-        moment_out[b] = backr[table[2 * SHARES + b]]
+        moment_out[b] = backr[table[2, b]]
         return 0
 
     lax.fori_loop(0, BLOCKS, place, 0)
@@ -361,50 +399,71 @@
 
     @pl.when(moves)
     def _():
-        remote(sendm.at[0:55], sendm.at[0:55], sems.at[2], recvm, peer).wait_send()
+        remote(sendm.at[0:55], sendm.at[0:55], sems.at[2], recvb, peer).wait_send()
         remote(backs.at[0:63], backs.at[0:63], sems.at[3], recvb, peer).wait_send()
 
     @pl.when(idle)
     def _():
-        remote(sendm.at[0:56], sendm.at[0:56], sems.at[2], recvm, peer).wait_send()
-
-
-def plan(owners, me):
-    blocks = jnp.arange(BLOCKS, dtype=jnp.int32)
-    shares = jnp.arange(SHARES, dtype=jnp.int32)
-    same = (owners[:, None] == owners[None, :]) & (blocks[None, :] < blocks[:, None])
-    rank = jnp.sum(same.astype(jnp.int32), axis=1)
-    idle = (shares >= 48) & (shares % 2 == 1)
-    mine = owners[None, :] == shares[:, None]
-    first = mine & (rank == 0)[None, :]
-    second = mine & (rank == 1)[None, :]
-    vacant = jnp.logical_not(jnp.any(mine, axis=1) | idle)
-    guest = (rank == 1) | ((owners >= 48) & (owners % 2 == 1))
-    vacant_at = jnp.sum(vacant[None, :] & (shares[None, :] < shares[:, None]), axis=1)
-    guest_at = jnp.sum(guest[None, :] & (blocks[None, :] < blocks[:, None]), axis=1)
-    hosted = vacant[:, None] & guest[None, :] & (vacant_at[:, None] == guest_at[None, :])
-    slot0 = jnp.sum(jnp.where(first | hosted, blocks[None, :], 0), axis=1)
-    slot1 = jnp.sum(jnp.where(second, blocks[None, :], 0), axis=1)
-    moved = hosted | (first & jnp.logical_not(idle)[:, None])
-    where = jnp.sum(jnp.where(moved, shares[:, None], 0), axis=0)
-    keeps = jnp.stack([jnp.any(owners == me), jnp.any((owners == me) & (rank == 1))])
-    return jnp.concatenate(
-        [slot0, slot1, jnp.pad(where, (0, SHARES - BLOCKS)), jnp.pad(keeps.astype(jnp.int32), (0, SHARES - 2))]
-    ).astype(jnp.int32)
+        remote(sendm.at[0:56], sendm.at[0:56], sems.at[2], recvb, peer).wait_send()
+
+
+def plan(owners, planned):
+    shape = (PANEL, PANEL)
+    sub = lax.broadcasted_iota(jnp.int32, shape, 0)
+    lane = lax.broadcasted_iota(jnp.int32, shape, 1)
+    column = jnp.broadcast_to(
+        jnp.concatenate([owners[...], jnp.full((PANEL - BLOCKS, 1), -1, jnp.int32)], axis=0), shape
+    )
+    row = column.T
+
+    def across(x):
+        return jnp.broadcast_to(jnp.sum(x.astype(jnp.int32), axis=1, keepdims=True), shape)
+
+    def down(x):
+        return jnp.broadcast_to(jnp.sum(x.astype(jnp.int32), axis=0, keepdims=True), shape)
+
+    def resting(t):
+        return ((t & 1) == 1) & (((t >> 1) & 3) == (t >> 4))
+
+    same = column == row
+    rank_c = across(same & (lane < sub))
+    rank_r = down(same & (sub < lane))
+    mine = column == lane
+    first = mine & (rank_c == 0)
+    second = mine & (rank_c == 1)
+    owned_r = down(mine)
+    owned_c = across(row == sub)
+    vacant_r = (owned_r == 0) & jnp.logical_not(resting(lane)) & (lane < SHARES)
+    vacant_c = (owned_c == 0) & jnp.logical_not(resting(sub)) & (sub < SHARES)
+    guest_c = (column >= 0) & ((rank_c == 1) | resting(column))
+    guest_r = (row >= 0) & ((rank_r == 1) | resting(row))
+    vacant_at = down(vacant_c & (sub < lane))
+    guest_at = across(guest_r & (lane < sub))
+    hosted = guest_c & vacant_r & (vacant_at == guest_at)
+    zero = jnp.zeros(shape, jnp.int32)
+    moved = hosted | (first & jnp.logical_not(resting(lane)))
+    rows = (
+        down(jnp.where(first | hosted, sub, zero)),
+        down(jnp.where(second, sub, zero)),
+        across(jnp.where(moved, lane, zero)).T,
+        owned_r,
+        down(second),
+    )
+    for i, x in enumerate(rows):
+        planned[i:i + 1, :] = x[0:1, :]
 
 
 def per_device(factor, old_basis, moment, owner_table):
-    me = lax.axis_index("fsdp") * 2 + lax.axis_index("own")
-    table = plan(owner_table[:, 0], me)
     bf16 = jnp.bfloat16
     vmem = pl.BlockSpec(memory_space=pltpu.VMEM)
+    hbm = pl.BlockSpec(memory_space=pl.ANY)
     return pl.pallas_call(
         refresh_kernel,
         out_shape=(
             jax.ShapeDtypeStruct(moment.shape, bf16),
             jax.ShapeDtypeStruct((1, SLOTS, ORDER, ORDER), bf16),
         ),
-        in_specs=[pl.BlockSpec(memory_space=pltpu.SMEM), vmem, vmem, vmem],
+        in_specs=[vmem, hbm, hbm, hbm],
         out_specs=(vmem, vmem),
         scratch_shapes=[
             pltpu.VMEM((SHARES, 8, FULL), bf16),
@@ -420,17 +479,23 @@
             pltpu.VMEM((PANEL, PANEL), jnp.float32),
             pltpu.VMEM((PANEL, PANEL), jnp.float32),
             pltpu.VMEM((ORDER, ORDER), bf16),
+            pltpu.VMEM(factor.shape, bf16),
+            pltpu.VMEM(old_basis.shape, bf16),
+            pltpu.VMEM(moment.shape, bf16),
+            pltpu.VMEM((8, PANEL), jnp.int32),
+            pltpu.SMEM((8, PANEL), jnp.int32),
             pltpu.SemaphoreType.DMA((4,)),
             pltpu.SemaphoreType.DMA((2,)),
             pltpu.SemaphoreType.DMA((2,)),
+            pltpu.SemaphoreType.DMA((2,)),
             pltpu.SemaphoreType.DMA,
-            pltpu.SemaphoreType.DMA,
+            pltpu.SemaphoreType.DMA((4,)),
         ],
         compiler_params=pltpu.CompilerParams(
-            collective_id=0, has_side_effects=True, vmem_limit_bytes=48 * 2**20
+            collective_id=0, has_side_effects=True, vmem_limit_bytes=60 * 2**20
         ),
         cost_estimate=pl.CostEstimate(flops=8 * 10**9, bytes_accessed=4 * 2**20, transcendentals=0),
-    )(table, factor, old_basis, moment)
+    )(owner_table, factor, old_basis, moment)
 
 
 def solution(mesh):

time: 113 us -> 102 us (0.903)
  the two profiles are of different devices: /device:TPU:1 before, /device:TPU:7 now
where the time goes in v3:
time: 102 us
  Pallas kernels  96.3 us (94%)
  local copies, waits for them, and re-layouts  4.57 us (4%)
    pallas_call x1, Pallas kernels, per_device(): pl.pallas_call(refresh_kernel, out_shape=(jax.ShapeDtypeStruct(moment.sha...  96.3 us
    unnamed x5, local copies, waits for them, and re-layouts  4.57 us

profile of v3, /device:TPU:7, one launch (start us, length us, event | category | flops | bytes accessed | tf_op | source)
XLA Modules:
  0.0 101.6 jit_solution(2137128695650548643)
XLA Ops:
  0.6 1.4 %copy.6.owners = s32[56,1]{1,0:T(8,128)} copy(s32[56,1]{0,1:T(1,128)} %param.7) | data formatting | bytes 448 | tf_op args[3]
  2.0 96.3 %shard_map.59 = (bf16[56,16,512]{2,1,0:T(8,128)(2,1)}, bf16[1,2,512,512]{3,2,1,0:T(8,128)(2,1)}) custom-call(s32[56,1]{1,0:T(8,128)} %copy.6.owners, bf16[56,8,512]{2,1,0:T(8,128)(2,1)} %factor_hbm.1, bf16[56,8,512]{2,1,0:T(8,128)(2,1)} %basis_hbm.1, bf16[56,16,512]{2,1,0:T(8,128)(2,1)} %moment_hbm.1), custom_call_target="tpu_custom_call" | custom-call | flops 8000000000 | bytes 4194304 | tf_op jit(solution)/shard_map/pallas_call | solution.py:460
  98.3 0.0 copy-start
  98.3 2.2 %copy.9 = bf16[56,16,512]{2,1,0:T(8,128)(2,1)} copy(bf16[56,16,512]{2,1,0:T(8,128)(2,1)} %get-tuple-element.4) | data formatting | bytes 1835008
  100.6 0.0 copy-done
  100.6 1.0 copy.10
Async XLA Ops:
  98.3 2.3 %copy-start = (bf16[1,2,512,512]{3,2,1,0:T(8,128)(2,1)S(1)}, bf16[1,2,512,512]{3,2,1,0:T(8,128)(2,1)}, u32[]{:S(2)}) copy-start(bf16[1,2,512,512]{3,2,1,0:T(8,128)(2,1)} %get-tuple-element.5) | copy-start | bytes 3145732

commit v4 on v3

v4 whole, which is shorter than its diff:
```python
import functools

import jax
import jax.numpy as jnp
from jax import lax
from jax.experimental import pallas as pl
from jax.experimental.pallas import tpu as pltpu
from jax.sharding import PartitionSpec as P

SLOTS = 2
SHARES = 64
BLOCKS = 56
ORDER = 512
PANEL = 128
WIDTHS = ((ORDER + 3 * PANEL, ORDER + 2 * PANEL), (ORDER + 2 * PANEL, ORDER + PANEL))
SUB = 32


def rows_of(v, s):
    return jnp.broadcast_to(v[s:s + 1, :], (8, 128))


def split(x):
    high = x.astype(jnp.bfloat16)
    return high, (x - high.astype(jnp.float32)).astype(jnp.bfloat16)


def left(x, axis):
    high, low = split(x)
    return jnp.concatenate([high, high, low], axis=axis)


def right(x):
    high, low = split(x)
    return jnp.concatenate([high, low, high], axis=0)


def dot_of(a, b, axis):
    return lax.dot_general(a, b, (((axis,), (0,)), ((), ())), preferred_element_type=jnp.float32)


def inverse_of(x):
    r = pl.reciprocal(x, approx=True)
    return r * (2.0 - x * r)


def factor_sub(wide, aug, at):
    tiles = SUB // 8
    wide, aug = list(wide), list(aug)
    sub = lax.broadcasted_iota(jnp.int32, (8, 128), 0)
    cols = {}
    for q in range(SUB):
        for t in range(q // 8, tiles):
            cols[q, t] = jnp.broadcast_to(wide[t][:, at + q:at + q + 1], (8, 128))
    diag = [None] * tiles
    mix = [None] * tiles
    for j in range(0, SUB, 2):
        tj, sj = j // 8, j % 8
        a = rows_of(cols[j, tj], sj)
        b = rows_of(cols[j, tj], sj + 1)
        d = rows_of(cols[j + 1, tj], sj + 1)
        det = a * d - b * b
        r = inverse_of(det)
        m0, m1 = {}, {}
        for t in range(tj, tiles):
            c0, c1 = cols[j, t], cols[j + 1, t]
            x0 = c0 * d - c1 * b
            x1 = c1 * a - c0 * b
            if t == tj:
                x0 = jnp.where(sub > sj + 1, x0, 0.0)
                x1 = jnp.where(sub > sj + 1, x1, 0.0)
            m0[t], m1[t] = x0 * r, x1 * r
        for q in range(j + 2, SUB):
            p0 = rows_of(cols[j, q // 8], q % 8)
            p1 = rows_of(cols[j + 1, q // 8], q % 8)
            for t in range(q // 8, tiles):
                cols[q, t] = cols[q, t] - (m0[t] * p0 + m1[t] * p1)
        w0, w1 = rows_of(wide[tj], sj), rows_of(wide[tj], sj + 1)
        x0, x1 = rows_of(aug[tj], sj), rows_of(aug[tj], sj + 1)
        for t in range(tj, tiles):
            wide[t] = wide[t] - m0[t] * w0 - m1[t] * w1
            aug[t] = aug[t] - m0[t] * x0 - m1[t] * x1
        ia = inverse_of(a)
        e = det * ia
        mu = b * ia
        if sj == 0:
            diag[tj] = jnp.where(sub == 0, a, e)
            mix[tj] = jnp.where(sub == 1, mu, 0.0)
        else:
            diag[tj] = jnp.where(sub == sj, a, jnp.where(sub == sj + 1, e, diag[tj]))
            mix[tj] = jnp.where(sub == sj + 1, mu, mix[tj])
    for t in range(tiles):
        s = lax.rsqrt(diag[t])
        wide[t] = s * (wide[t] - mix[t] * pltpu.roll(wide[t], 1, 0))
        aug[t] = s * (aug[t] - mix[t] * pltpu.roll(aug[t], 1, 0))
    return wide, aug


def dot_t(a, b):
    return dot_of(left(a, 0), right(b), 0)


def factor_block(diags, augs):
    r = lax.broadcasted_iota(jnp.int32, (128, 128), 0)
    c = lax.broadcasted_iota(jnp.int32, (128, 128), 1)
    for x in augs:
        x[...] = (r == c).astype(jnp.float32)
    for i in range(128 // SUB):
        for s, x in zip(diags, augs):
            at = SUB * i
            wide = [s[at + 8 * t:at + 8 * t + 8, :] for t in range(SUB // 8)]
            aug = [x[at + 8 * t:at + 8 * t + 8, :] for t in range(SUB // 8)]
            wide, aug = factor_sub(wide, aug, at)
            for t in range(SUB // 8):
                x[at + 8 * t:at + 8 * t + 8, :] = aug[t]
            if i < 128 // SUB - 1:
                u = jnp.concatenate(wide, axis=0)
                both = right(jnp.concatenate([u, jnp.concatenate(aug, axis=0)], axis=1))
                turned = left(u, 0)
                nx = at + SUB
                upd = dot_of(turned[:, nx:], both, 0)
                s[nx:, :] = s[nx:, :] - upd[:, :128]
                x[nx:, :] = x[nx:, :] - upd[:, 128:]


def at_share(t):
    return {"fsdp": t // 2, "own": lax.rem(t, 2)}


def share(x, y, c):
    return x * 16 + lax.rem(y + 8, 8) * 2 + c


def remote(src, dst, send, recv, t):
    return pltpu.make_async_remote_copy(
        src_ref=src,
        dst_ref=dst,
        send_sem=send,
        recv_sem=recv,
        device_id=at_share(t),
        device_id_type=pl.DeviceIdType.MESH,
    )


def is_idle(t):
    return (lax.rem(t, 2) == 1) & (lax.rem(t // 2, 4) == t // 16)


def wide_f32(x):
    return x.astype(jnp.float32).reshape(-1, x.shape[-1])


def refresh_kernel(
    owners,
    factor_hbm,
    basis_hbm,
    moment_hbm,
    moment_out,
    owner_basis,
    send0,
    send1,
    sendm,
    got0,
    got1,
    gotm,
    backs,
    backr,
    old,
    work,
    diag,
    inverse,
    rots,
    factor,
    basis,
    moment,
    planned,
    table,
    sent,
    recv0,
    recv1,
    recvm,
    recvr,
    recvb,
    local,
):
    fetches = [
        pltpu.make_async_copy(src, dst, local.at[i])
        for i, (src, dst) in enumerate(
            ((basis_hbm, basis), (factor_hbm, factor), (moment_hbm, moment))
        )
    ]
    for fetch in fetches:
        fetch.start()

    me = lax.axis_index("fsdp") * 2 + lax.axis_index("own")
    panel = me // 16
    line = lax.rem(me // 2, 8)
    core = lax.rem(me, 2)
    seat = panel * 2 + core
    peer = lax.rem(me + 1, SHARES)
    hosts = (me, share(panel, line - 1, core), share(panel, line + 1, core))
    active = [jnp.logical_not(is_idle(t)) for t in hosts]
    few = active[0] & active[1] & active[2]
    short = ((panel < 2) & (core == 1), (panel >= 2) & (core == 0))

    barrier = pltpu.get_barrier_semaphore()

    def greet(k, _):
        pl.semaphore_signal(
            barrier,
            inc=1,
            device_id=at_share(lax.rem(me + k, SHARES)),
            device_id_type=pl.DeviceIdType.MESH,
        )
        return 0

    lax.fori_loop(1, SHARES, greet, 0)

    plan(owners, planned)
    tables = pltpu.make_async_copy(planned, table, local.at[3])
    tables.start()
    for fetch in fetches[:2]:
        fetch.wait()
    tables.wait()

    def piece(b, turn):
        lane = pl.multiple_of(lax.rem(panel + turn, 4) * PANEL, PANEL)
        return factor[b, :, pl.ds(lane, PANEL)]

    tile_lane = lax.broadcasted_iota(jnp.int32, (8, PANEL), 1)
    odd = ((tile_lane >> 3) & 1) == 1
    whole_diag = jnp.logical_not(odd) | (jnp.full((8, PANEL), core, jnp.int32) == 1)
    whole_far = odd | (jnp.full((8, PANEL), panel, jnp.int32) < 2)

    def merge(mask, mine, other, turn):
        turned = pltpu.roll(other.astype(jnp.float32), turn, 1)
        return jnp.where(mask, mine.astype(jnp.float32), turned).astype(jnp.bfloat16)

    def pack0(t):
        a, b = table[0, t], table[1, t]
        send0[t, :, :ORDER] = basis[a]
        send0[t, :, ORDER:ORDER + PANEL] = piece(a, 1)
        send0[t, :, ORDER + PANEL:ORDER + 2 * PANEL] = merge(whole_diag, piece(a, 0), piece(b, 0), 8)
        send0[t, :, ORDER + 2 * PANEL:] = merge(whole_far, piece(a, 2), piece(b, 2), PANEL - 8)

    def pack1(t):
        b = table[1, t]
        send1[t, :, :ORDER] = basis[b]
        send1[t, :, ORDER:ORDER + PANEL] = piece(b, 1)
        send1[t, :, ORDER + PANEL:] = piece(b, 2 * (1 - core))

    def post(slot, pack, send, got, recv):
        long_width, short_width = WIDTHS[slot]

        def body(k, _):
            t = lax.rem(me + k, SHARES)
            pack(t)

            @pl.when(jnp.logical_not(short[slot]))
            def _():
                remote(send.at[t], got.at[me], sent.at[slot], recv.at[0], t).start()

            @pl.when(short[slot])
            def _():
                remote(
                    send.at[t, :, :short_width],
                    got.at[me, :, :short_width],
                    sent.at[slot],
                    recv.at[1],
                    t,
                ).start()

            return 0

        lax.fori_loop(1, SHARES, body, 0)
        pack(me)
        got[me] = send[me]

    def arrive(slot, got, recv):
        long_width, short_width = WIDTHS[slot]

        def take(longs, shorts):
            part = got.at[0:longs]
            remote(part, part, recv.at[0], recv.at[0], peer).wait_recv()
            part = got.at[0:shorts, :, :short_width]
            remote(part, part, recv.at[1], recv.at[1], peer).wait_recv()

        @pl.when(jnp.logical_not(short[slot]))
        def _():
            take(47, 16)

        @pl.when(short[slot])
        def _():
            take(48, 15)

    def flush(slot, send):
        long_width, short_width = WIDTHS[slot]

        @pl.when(jnp.logical_not(short[slot]))
        def _():
            part = send.at[0:63]
            remote(part, part, sent.at[slot], recvb, peer).wait_send()

        @pl.when(short[slot])
        def _():
            part = send.at[0:63, :, :short_width]
            remote(part, part, sent.at[slot], recvb, peer).wait_send()

    def route(t):
        gap = lax.rem(line - lax.rem(t // 2, 8) + 8, 8)
        above = (gap > 0) & ((gap < 4) | ((gap == 4) & (core == 0)))
        region = jnp.where(gap == 0, 0, jnp.where(above, 1, 2))
        dest = share(t // 16, lax.rem(t // 2, 8) + jnp.where(region == 2, 7, region), lax.rem(t, 2))
        place = jnp.where(gap == 0, 0, jnp.where(above, gap, 12 - gap)) * 8 + seat
        return dest, region, place

    def postm(k, _):
        t = lax.rem(me + k, SHARES)
        sendm[t] = moment[table[0, t]]
        dest, region, place = route(t)

        @pl.when((dest != me) & jnp.logical_not(is_idle(t)))
        def _():
            remote(sendm.at[t], gotm.at[place], sent.at[2], recvm.at[region], dest).start()

        return 0

    def load(slot):
        got = (got0, got1)[slot]
        whole = wide_f32(got[:, :, :ORDER]).astype(jnp.bfloat16)
        old[...] = whole
        row_odd = ((lax.broadcasted_iota(jnp.int32, (PANEL, PANEL), 0) >> 3) & 1) == 1
        lane_odd = ((lax.broadcasted_iota(jnp.int32, (PANEL, PANEL), 1) >> 3) & 1) == 1

        def tile(ref, p, q):
            lo = ORDER + q * PANEL
            return wide_f32(ref[16 * p:16 * p + 16, :, lo:lo + PANEL])

        part = {}
        for p in range(4):
            q = (p + 1) % 4
            part[p, q] = tile(got, p, 0)
            part[q, p] = part[p, q].T
            own = tile(got0, p, 1)
            if slot == 1:
                own = jnp.where(row_odd, tile(got1, p, 1), pltpu.roll(own, PANEL - 8, 1))
            part[p, p] = jnp.where(row_odd | jnp.logical_not(lane_odd), own, own.T)
        for p in range(2):
            near, far = tile(got0, p, 2), tile(got0, p + 2, 2)
            if slot == 1:
                near, far = tile(got1, p, 1), pltpu.roll(far, 8, 1)
            part[p, p + 2] = jnp.where(row_odd, far.T, near)
            part[p + 2, p] = part[p, p + 2].T
        full = jnp.concatenate(
            [jnp.concatenate([part[p, q] for q in range(4)], axis=1) for p in range(4)], axis=0
        ).astype(jnp.bfloat16)
        pt = lax.dot_general(
            whole, full, (((0,), (0,)), ((), ())), preferred_element_type=jnp.float32
        ).astype(jnp.bfloat16)
        work[:, :ORDER] = lax.dot_general(
            pt, pt, (((1,), (1,)), ((), ())), preferred_element_type=jnp.float32
        )
        work[:, ORDER:] = pt.astype(jnp.float32)

    def panel_step(k):
        at = pl.multiple_of(k * PANEL, PANEL)
        diag[...] = work[pl.ds(at, PANEL), pl.ds(at, PANEL)]
        factor_block([diag], [inverse])
        work[pl.ds(at, PANEL), :] = dot_of(
            left(inverse[...], 1), right(work[pl.ds(at, PANEL), :]), 1
        )
        for kk in range(3):

            @pl.when(k == kk)
            def _():
                lo = PANEL * (kk + 1)
                u = work[lo - PANEL:lo, lo:ORDER]
                work[lo:, lo:] = work[lo:, lo:] - dot_t(u, work[lo - PANEL:lo, lo:])

    def keep(slot):
        there = jnp.full((ORDER, ORDER), table[3 + slot, me], jnp.int32)
        owner_basis[0, slot] = jnp.where(there > 0, work[:, ORDER:].T, 0.0).astype(jnp.bfloat16)

    def rotate(region, low, high):
        host = hosts[region]

        def group(g, _):
            rows = pl.ds(pl.multiple_of(g * 8, 8), 8)
            x = gotm[rows].reshape(8 * 16, ORDER)
            y = jnp.dot(x, rots[region], preferred_element_type=jnp.float32).astype(jnp.bfloat16)
            backs[rows] = y.reshape(8, 16, ORDER)
            away = g - low
            place = line + (away if region == 1 else -away)

            def reply(k, _):
                t = share(k // 2, place, lax.rem(k, 2))
                ours = jnp.logical_or(away < 3, lax.rem(k, 2) == region - 1)

                @pl.when((t != me) & ours)
                def _():
                    remote(
                        backs.at[g * 8 + k], backr.at[host], sent.at[3 + region], recvb, t
                    ).start()

                return 0

            lax.fori_loop(0, 8, reply, 0)
            return 0

        lax.fori_loop(low, high, group, 0)
        backr[host] = backs[low * 8 + seat]

    def took(region, wait_in):
        part = gotm.at[0:7] if region == 0 else gotm.at[0:27]
        if wait_in:
            remote(part, part, sent.at[2], recvm.at[region], peer).wait_recv()
        else:
            remote(part, part, sent.at[3 + region], recvb, peer).wait_send()

    def post_moments():
        lax.fori_loop(0, SHARES, postm, 0)
        for region in range(3):
            gotm[(0, 8, 40)[region] + seat] = sendm[hosts[region]]

    pl.semaphore_wait(barrier, SHARES - 1)
    post(0, pack0, send0, got0, recv0)
    post(1, pack1, send1, got1, recv1)
    fetches[2].wait()
    if 0 < 0:
        post_moments()

    def step(i, _):
        @pl.when(i == 0)
        def _():
            arrive(0, got0, recv0)
            if 0 == 0:
                post_moments()
            load(0)

        if 0 > 0:

            @pl.when(i == 0)
            def _():
                post_moments()

        @pl.when(i == 4)
        def _():
            keep(0)

            @pl.when(active[0])
            def _():
                rots[0] = lax.dot_general(
                    old[...],
                    work[:, ORDER:].astype(jnp.bfloat16),
                    (((0,), (1,)), ((), ())),
                    preferred_element_type=jnp.float32,
                ).astype(jnp.bfloat16)
                for q in range(4):
                    rows = pl.ds(q * PANEL, PANEL)
                    for side in range(2):
                        remote(
                            rots.at[0, rows],
                            rots.at[2 - side, rows],
                            sent.at[6],
                            recvr.at[1 - side],
                            hosts[1 + side],
                        ).start()

            arrive(1, got1, recv1)
            load(1)

        @pl.when((i == 5) & active[0])
        def _():
            took(0, True)
            rotate(0, 0, 1)

        for region in (1, 2):

            @pl.when((i == 6) & active[region])
            def _():
                took(region, True)
                remote(rots.at[0], rots.at[region], sent.at[6], recvr.at[region - 1], peer).wait_recv()
                rotate(region, 4 * region - 3, 4 * region + 1)

        panel_step(lax.rem(i, 4))
        return 0

    lax.fori_loop(0, 8, step, 0)
    keep(1)

    @pl.when(few)
    def _():
        remote(backr.at[0:53], backr.at[0:53], sent.at[2], recvb, peer).wait_recv()

    @pl.when(jnp.logical_not(few))
    def _():
        remote(backr.at[0:54], backr.at[0:54], sent.at[2], recvb, peer).wait_recv()

    def place(b, _):
        moment_out[b] = backr[table[2, b]]
        return 0

    lax.fori_loop(0, BLOCKS, place, 0)

    flush(0, send0)
    flush(1, send1)

    @pl.when(few)
    def _():
        remote(sendm.at[0:53], sendm.at[0:53], sent.at[2], recvb, peer).wait_send()

    @pl.when(jnp.logical_not(few))
    def _():
        remote(sendm.at[0:54], sendm.at[0:54], sent.at[2], recvb, peer).wait_send()

    for region in range(3):

        @pl.when(active[region])
        def _():
            took(region, False)

    @pl.when(active[0])
    def _():
        remote(rots.at[0:2], rots.at[0:2], sent.at[6], recvb, peer).wait_send()


def plan(owners, planned):
    shape = (PANEL, PANEL)
    sub = lax.broadcasted_iota(jnp.int32, shape, 0)
    lane = lax.broadcasted_iota(jnp.int32, shape, 1)
    row = jnp.broadcast_to(
        jnp.concatenate([owners[...], jnp.full((1, PANEL - BLOCKS), -1, jnp.int32)], axis=1), shape
    )
    column = row.T

    def across(x):
        return jnp.broadcast_to(jnp.sum(x.astype(jnp.int32), axis=1, keepdims=True), shape)

    def down(x):
        return jnp.broadcast_to(jnp.sum(x.astype(jnp.int32), axis=0, keepdims=True), shape)

    def resting(t):
        return ((t & 1) == 1) & (((t >> 1) & 3) == (t >> 4))

    same = column == row
    rank_c = across(same & (lane < sub))
    rank_r = down(same & (sub < lane))
    mine = column == lane
    first = mine & (rank_c == 0)
    second = mine & (rank_c == 1)
    owned_r = down(mine)
    owned_c = across(row == sub)
    vacant_r = (owned_r == 0) & jnp.logical_not(resting(lane)) & (lane < SHARES)
    vacant_c = (owned_c == 0) & jnp.logical_not(resting(sub)) & (sub < SHARES)
    guest_c = (column >= 0) & ((rank_c == 1) | resting(column))
    guest_r = (row >= 0) & ((rank_r == 1) | resting(row))
    vacant_at = down(vacant_c & (sub < lane))
    guest_at = across(guest_r & (lane < sub))
    hosted = guest_c & vacant_r & (vacant_at == guest_at)
    zero = jnp.zeros(shape, jnp.int32)
    moved = hosted | (first & jnp.logical_not(resting(lane)))
    rows = (
        down(jnp.where(first | hosted, sub, zero)),
        down(jnp.where(second, sub, zero)),
        across(jnp.where(moved, lane, zero)).T,
        owned_r,
        down(second),
    )
    planned[...] = jnp.zeros(planned.shape, jnp.int32)
    for i, x in enumerate(rows):
        planned[i:i + 1, :] = x[0:1, :]


def per_device(factor, old_basis, moment, owner_table):
    bf16 = jnp.bfloat16
    vmem = pl.BlockSpec(memory_space=pltpu.VMEM)
    hbm = pl.BlockSpec(memory_space=pl.ANY)
    return pl.pallas_call(
        refresh_kernel,
        out_shape=(
            jax.ShapeDtypeStruct(moment.shape, bf16),
            jax.ShapeDtypeStruct((1, SLOTS, ORDER, ORDER), bf16),
        ),
        in_specs=[vmem, hbm, hbm, hbm],
        out_specs=(vmem, vmem),
        scratch_shapes=[
            pltpu.VMEM((SHARES, 8, WIDTHS[0][0]), bf16),
            pltpu.VMEM((SHARES, 8, WIDTHS[1][0]), bf16),
            pltpu.VMEM((SHARES, 16, ORDER), bf16),
            pltpu.VMEM((SHARES, 8, WIDTHS[0][0]), bf16),
            pltpu.VMEM((SHARES, 8, WIDTHS[1][0]), bf16),
            pltpu.VMEM((72, 16, ORDER), bf16),
            pltpu.VMEM((72, 16, ORDER), bf16),
            pltpu.VMEM((SHARES, 16, ORDER), bf16),
            pltpu.VMEM((ORDER, ORDER), bf16),
            pltpu.VMEM((ORDER, 2 * ORDER), jnp.float32),
            pltpu.VMEM((PANEL, PANEL), jnp.float32),
            pltpu.VMEM((PANEL, PANEL), jnp.float32),
            pltpu.VMEM((3, ORDER, ORDER), bf16),
            pltpu.VMEM(factor.shape, bf16),
            pltpu.VMEM(old_basis.shape, bf16),
            pltpu.VMEM(moment.shape, bf16),
            pltpu.VMEM((8, PANEL), jnp.int32),
            pltpu.SMEM((8, PANEL), jnp.int32),
            pltpu.SemaphoreType.DMA((7,)),
            pltpu.SemaphoreType.DMA((2,)),
            pltpu.SemaphoreType.DMA((2,)),
            pltpu.SemaphoreType.DMA((3,)),
            pltpu.SemaphoreType.DMA((2,)),
            pltpu.SemaphoreType.DMA,
            pltpu.SemaphoreType.DMA((4,)),
        ],
        compiler_params=pltpu.CompilerParams(
            collective_id=0, has_side_effects=True, vmem_limit_bytes=60 * 2**20
        ),
        cost_estimate=pl.CostEstimate(flops=8 * 10**9, bytes_accessed=4 * 2**20, transcendentals=0),
    )(owner_table.reshape(1, BLOCKS), factor, old_basis, moment)


def solution(mesh):
    in_specs = (
        P("layer", ("fsdp", "own"), None),
        P("layer", ("fsdp", "own"), None),
        P("layer", ("fsdp", "own"), None),
        P("layer", None),
    )
    out_specs = (P("layer", ("fsdp", "own"), None), P("layer", ("fsdp", "own"), None, None))
    return jax.shard_map(
        per_device, mesh=mesh, in_specs=in_specs, out_specs=out_specs, check_vma=False
    )
```

time: 102 us -> 95.3 us (0.934)
  the two profiles are of different devices: /device:TPU:7 before, /device:TPU:1 now
where the time goes in v4:
time: 95.3 us; the launch traced here: 95.2 us
  Pallas kernels  91.3 us (96%)
  local copies, waits for them, and re-layouts  3.22 us (3%)
    pallas_call x1, Pallas kernels, per_device(): pl.pallas_call(refresh_kernel, out_shape=(jax.ShapeDtypeStruct(moment.sha...  91.3 us
    unnamed x4, local copies, waits for them, and re-layouts  3.22 us

profile of v4, /device:TPU:1, one launch (start us, length us, event | category | flops | bytes accessed | tf_op | source)
XLA Modules:
  0.0 95.2 jit_solution(17728373171237651235)
XLA Ops:
  0.6 91.3 %shard_map.59 = (bf16[56,16,512]{2,1,0:T(8,128)(2,1)}, bf16[1,2,512,512]{3,2,1,0:T(8,128)(2,1)}) custom-call(s32[1,56]{1,0:T(1,128)} %bitcast.1, bf16[56,8,512]{2,1,0:T(8,128)(2,1)} %factor_hbm.1, bf16[56,8,512]{2,1,0:T(8,128)(2,1)} %basis_hbm.1, bf16[56,16,512]{2,1,0:T(8,128)(2,1)} %moment_hbm.1), custom_call_target="tpu_custom_call" | custom-call | flops 8000000000 | bytes 4194304 | tf_op jit(solution)/shard_map/pallas_call | solution.py:578
  91.9 0.0 copy-start
  91.9 2.2 %copy.8 = bf16[56,16,512]{2,1,0:T(8,128)(2,1)} copy(bf16[56,16,512]{2,1,0:T(8,128)(2,1)} %get-tuple-element.4) | data formatting | bytes 1835008
  94.2 0.0 copy-done
  94.2 1.0 %copy.9 = bf16[1,2,512,512]{3,2,1,0:T(8,128)(2,1)} copy(bf16[1,2,512,512]{3,2,1,0:T(8,128)(2,1)S(1)} %copy-done) | data formatting | bytes 2097152
Async XLA Ops:
  91.9 2.3 %copy-start = (bf16[1,2,512,512]{3,2,1,0:T(8,128)(2,1)S(1)}, bf16[1,2,512,512]{3,2,1,0:T(8,128)(2,1)}, u32[]{:S(2)}) copy-start(bf16[1,2,512,512]{3,2,1,0:T(8,128)(2,1)} %get-tuple-element.5) | copy-start | bytes 3145732

commit v5 on v4

--- a/solution.py
+++ b/solution.py
@@ -146,6 +146,9 @@
     return (lax.rem(t, 2) == 1) & (lax.rem(t // 2, 4) == t // 16)
 
 
+FIRST = (0, 1, 5)
+
+
 def wide_f32(x):
     return x.astype(jnp.float32).reshape(-1, x.shape[-1])
 
@@ -155,8 +158,9 @@
     factor_hbm,
     basis_hbm,
     moment_hbm,
-    moment_out,
+    backr,
     owner_basis,
+    planned,
     send0,
     send1,
     sendm,
@@ -164,7 +168,7 @@
     got1,
     gotm,
     backs,
-    backr,
+    kept,
     old,
     work,
     diag,
@@ -173,7 +177,6 @@
     factor,
     basis,
     moment,
-    planned,
     table,
     sent,
     recv0,
@@ -191,6 +194,10 @@
     ]
     for fetch in fetches:
         fetch.start()
+    stores = [
+        pltpu.make_async_copy(kept.at[slot], owner_basis.at[0, slot], local.at[4 + slot])
+        for slot in range(SLOTS)
+    ]
 
     me = lax.axis_index("fsdp") * 2 + lax.axis_index("own")
     panel = me // 16
@@ -327,8 +334,7 @@
 
     def load(slot):
         got = (got0, got1)[slot]
-        whole = wide_f32(got[:, :, :ORDER]).astype(jnp.bfloat16)
-        old[...] = whole
+        old[...] = wide_f32(got[:, :, :ORDER]).T.astype(jnp.bfloat16)
         row_odd = ((lax.broadcasted_iota(jnp.int32, (PANEL, PANEL), 0) >> 3) & 1) == 1
         lane_odd = ((lax.broadcasted_iota(jnp.int32, (PANEL, PANEL), 1) >> 3) & 1) == 1
 
@@ -354,9 +360,7 @@
         full = jnp.concatenate(
             [jnp.concatenate([part[p, q] for q in range(4)], axis=1) for p in range(4)], axis=0
         ).astype(jnp.bfloat16)
-        pt = lax.dot_general(
-            whole, full, (((0,), (0,)), ((), ())), preferred_element_type=jnp.float32
-        ).astype(jnp.bfloat16)
+        pt = jnp.dot(old[...], full, preferred_element_type=jnp.float32).astype(jnp.bfloat16)
         work[:, :ORDER] = lax.dot_general(
             pt, pt, (((1,), (1,)), ((), ())), preferred_element_type=jnp.float32
         )
@@ -379,42 +383,101 @@
 
     def keep(slot):
         there = jnp.full((ORDER, ORDER), table[3 + slot, me], jnp.int32)
-        owner_basis[0, slot] = jnp.where(there > 0, work[:, ORDER:].T, 0.0).astype(jnp.bfloat16)
-
-    def rotate(region, low, high):
-        host = hosts[region]
-
-        def group(g, _):
-            rows = pl.ds(pl.multiple_of(g * 8, 8), 8)
-            x = gotm[rows].reshape(8 * 16, ORDER)
-            y = jnp.dot(x, rots[region], preferred_element_type=jnp.float32).astype(jnp.bfloat16)
-            backs[rows] = y.reshape(8, 16, ORDER)
-            away = g - low
-            place = line + (away if region == 1 else -away)
-
-            def reply(k, _):
-                t = share(k // 2, place, lax.rem(k, 2))
-                ours = jnp.logical_or(away < 3, lax.rem(k, 2) == region - 1)
-
-                @pl.when((t != me) & ours)
+        kept[slot] = jnp.where(there > 0, work[:, ORDER:].T, 0.0).astype(jnp.bfloat16)
+        stores[slot].start()
+
+    def turn(k):
+        at = pl.multiple_of(k * PANEL, PANEL)
+        rots[0, k] = lax.dot_general(
+            old[...],
+            work[pl.ds(at, PANEL), ORDER:].astype(jnp.bfloat16),
+            (((1,), (1,)), ((), ())),
+            preferred_element_type=jnp.float32,
+        ).astype(jnp.bfloat16)
+        for side in range(2):
+            remote(
+                rots.at[0, k], rots.at[2 - side, k], sent.at[6], recvr.at[1 - side, k], hosts[1 + side]
+            ).start()
+
+    def turned(region, half):
+        for k in (2 * half, 2 * half + 1):
+            remote(
+                rots.at[0, k], rots.at[region, k], sent.at[6], recvr.at[region - 1, k], peer
+            ).wait_recv()
+
+    def local_reply(region, half):
+        return pltpu.make_async_copy(
+            backs.at[half, FIRST[region] * 8 + seat],
+            backr.at[half, hosts[region]],
+            local.at[6 + 2 * region + half],
+        )
+
+    def rotate(region, half, away):
+        g = FIRST[region] + away
+        rows = pl.ds(pl.multiple_of(g * 8, 8), 8)
+        x = gotm[rows].reshape(8 * 16, ORDER)
+        r = jnp.concatenate([rots[region, 2 * half], rots[region, 2 * half + 1]], axis=1)
+        y = jnp.dot(x, r, preferred_element_type=jnp.float32).astype(jnp.bfloat16)
+        backs[half, rows] = y.reshape(8, 16, 2 * PANEL)
+        place = line + (away if region == 1 else -away)
+
+        def reply(k, _):
+            t = share(k // 2, place, lax.rem(k, 2))
+            ours = jnp.logical_or(away < 3, lax.rem(k, 2) == region - 1)
+
+            @pl.when((t != me) & ours)
+            def _():
+                remote(
+                    backs.at[half, g * 8 + k],
+                    backr.at[half, hosts[region]],
+                    sent.at[3 + region],
+                    recvb,
+                    t,
+                ).start()
+
+            return 0
+
+        lax.fori_loop(0, 8, reply, 0)
+
+    def rotate_half(half):
+        @pl.when(active[0])
+        def _():
+            if half == 0:
+                took(0, True)
+            rotate(0, half, 0)
+            local_reply(0, half).start()
+
+        for region in (1, 2):
+
+            @pl.when(active[region])
+            def _():
+                if half == 0:
+                    took(region, True)
+                turned(region, half)
+
+        def pair(away, _):
+            for region in (1, 2):
+
+                @pl.when(active[region])
                 def _():
-                    remote(
-                        backs.at[g * 8 + k], backr.at[host], sent.at[3 + region], recvb, t
-                    ).start()
-
-                return 0
-
-            lax.fori_loop(0, 8, reply, 0)
+                    rotate(region, half, away)
+
             return 0
 
-        lax.fori_loop(low, high, group, 0)
-        backr[host] = backs[low * 8 + seat]
+        lax.fori_loop(0, 4, pair, 0)
+        for region in (1, 2):
+
+            @pl.when(active[region])
+            def _():
+                local_reply(region, half).start()
 
     def took(region, wait_in):
-        part = gotm.at[0:7] if region == 0 else gotm.at[0:27]
+        count = 7 if region == 0 else 27
         if wait_in:
+            part = gotm.at[0:count]
             remote(part, part, sent.at[2], recvm.at[region], peer).wait_recv()
         else:
+            part = backs.at[:, 0:count]
             remote(part, part, sent.at[3 + region], recvb, peer).wait_send()
 
     def post_moments():
@@ -426,63 +489,33 @@
     post(0, pack0, send0, got0, recv0)
     post(1, pack1, send1, got1, recv1)
     fetches[2].wait()
-    if 0 < 0:
-        post_moments()
+    post_moments()
 
     def step(i, _):
         @pl.when(i == 0)
         def _():
             arrive(0, got0, recv0)
-            if 0 == 0:
-                post_moments()
             load(0)
 
-        if 0 > 0:
-
-            @pl.when(i == 0)
-            def _():
-                post_moments()
-
         @pl.when(i == 4)
         def _():
             keep(0)
-
-            @pl.when(active[0])
-            def _():
-                rots[0] = lax.dot_general(
-                    old[...],
-                    work[:, ORDER:].astype(jnp.bfloat16),
-                    (((0,), (1,)), ((), ())),
-                    preferred_element_type=jnp.float32,
-                ).astype(jnp.bfloat16)
-                for q in range(4):
-                    rows = pl.ds(q * PANEL, PANEL)
-                    for side in range(2):
-                        remote(
-                            rots.at[0, rows],
-                            rots.at[2 - side, rows],
-                            sent.at[6],
-                            recvr.at[1 - side],
-                            hosts[1 + side],
-                        ).start()
 
             arrive(1, got1, recv1)
             load(1)
 
-        @pl.when((i == 5) & active[0])
-        def _():
-            took(0, True)
-            rotate(0, 0, 1)
-
-        for region in (1, 2):
-
-            @pl.when((i == 6) & active[region])
+        for half in range(2):
+
+            @pl.when(i == 5 + half)
             def _():
-                took(region, True)
-                remote(rots.at[0], rots.at[region], sent.at[6], recvr.at[region - 1], peer).wait_recv()
-                rotate(region, 4 * region - 3, 4 * region + 1)
+                rotate_half(half)
 
         panel_step(lax.rem(i, 4))
+
+        @pl.when((i < 4) & active[0])
+        def _():
+            turn(lax.rem(i, 4))
+
         return 0
 
     lax.fori_loop(0, 8, step, 0)
@@ -490,17 +523,13 @@
 
     @pl.when(few)
     def _():
-        remote(backr.at[0:53], backr.at[0:53], sent.at[2], recvb, peer).wait_recv()
+        part = backr.at[:, 0:53]
+        remote(part, part, sent.at[2], recvb, peer).wait_recv()
 
     @pl.when(jnp.logical_not(few))
     def _():
-        remote(backr.at[0:54], backr.at[0:54], sent.at[2], recvb, peer).wait_recv()
-
-    def place(b, _):
-        moment_out[b] = backr[table[2, b]]
-        return 0
-
-    lax.fori_loop(0, BLOCKS, place, 0)
+        part = backr.at[:, 0:54]
+        remote(part, part, sent.at[2], recvb, peer).wait_recv()
 
     flush(0, send0)
     flush(1, send1)
@@ -518,6 +547,11 @@
         @pl.when(active[region])
         def _():
             took(region, False)
+            for half in range(2):
+                local_reply(region, half).wait()
+
+    for store in stores:
+        store.wait()
 
     @pl.when(active[0])
     def _():
@@ -571,18 +605,61 @@
         planned[i:i + 1, :] = x[0:1, :]
 
 
+def place_kernel(table, backs, kept, moment_out, owner_basis, rows, bases, sems):
+    parts = SHARES // 16
+    loads, bases_in, bases_out = [], [], []
+    for q in range(parts):
+        cut = slice(16 * q, 16 * q + 16)
+        loads.append(pltpu.make_async_copy(backs.at[:, cut], rows.at[:, cut], sems.at[q]))
+        loads[q].start()
+    for slot in range(SLOTS):
+        bases_in.append(
+            pltpu.make_async_copy(kept.at[0, slot], bases.at[slot], sems.at[parts + slot])
+        )
+        bases_out.append(
+            pltpu.make_async_copy(
+                bases.at[slot], owner_basis.at[0, slot], sems.at[parts + SLOTS + slot]
+            )
+        )
+        bases_in[slot].start()
+
+    def place(t, _):
+        @pl.when(jnp.logical_not(is_idle(t)))
+        def _():
+            for half in range(2):
+                pltpu.make_async_copy(
+                    rows.at[half, t],
+                    moment_out.at[table[0, t], :, 2 * PANEL * half:2 * PANEL * (half + 1)],
+                    sems.at[parts + 2 * SLOTS],
+                ).start()
+
+        return 0
+
+    for q in range(parts):
+        loads[q].wait()
+        lax.fori_loop(16 * q, 16 * q + 16, place, 0)
+    for slot in range(SLOTS):
+        bases_in[slot].wait()
+        bases_out[slot].start()
+    pltpu.make_async_copy(moment_out, moment_out, sems.at[parts + 2 * SLOTS]).wait()
+    for slot in range(SLOTS):
+        bases_out[slot].wait()
+
+
 def per_device(factor, old_basis, moment, owner_table):
     bf16 = jnp.bfloat16
     vmem = pl.BlockSpec(memory_space=pltpu.VMEM)
     hbm = pl.BlockSpec(memory_space=pl.ANY)
-    return pl.pallas_call(
+    kept = jax.ShapeDtypeStruct((1, SLOTS, ORDER, ORDER), bf16)
+    backs, bases, table = pl.pallas_call(
         refresh_kernel,
         out_shape=(
-            jax.ShapeDtypeStruct(moment.shape, bf16),
-            jax.ShapeDtypeStruct((1, SLOTS, ORDER, ORDER), bf16),
+            jax.ShapeDtypeStruct((2, SHARES, 16, 2 * PANEL), bf16),
+            kept,
+            jax.ShapeDtypeStruct((8, PANEL), jnp.int32),
         ),
         in_specs=[vmem, hbm, hbm, hbm],
-        out_specs=(vmem, vmem),
+        out_specs=(hbm, hbm, vmem),
         scratch_shapes=[
             pltpu.VMEM((SHARES, 8, WIDTHS[0][0]), bf16),
             pltpu.VMEM((SHARES, 8, WIDTHS[1][0]), bf16),
@@ -590,31 +667,42 @@
             pltpu.VMEM((SHARES, 8, WIDTHS[0][0]), bf16),
             pltpu.VMEM((SHARES, 8, WIDTHS[1][0]), bf16),
             pltpu.VMEM((72, 16, ORDER), bf16),
-            pltpu.VMEM((72, 16, ORDER), bf16),
-            pltpu.VMEM((SHARES, 16, ORDER), bf16),
+            pltpu.VMEM((2, 72, 16, 2 * PANEL), bf16),
+            pltpu.VMEM((SLOTS, ORDER, ORDER), bf16),
             pltpu.VMEM((ORDER, ORDER), bf16),
             pltpu.VMEM((ORDER, 2 * ORDER), jnp.float32),
             pltpu.VMEM((PANEL, PANEL), jnp.float32),
             pltpu.VMEM((PANEL, PANEL), jnp.float32),
-            pltpu.VMEM((3, ORDER, ORDER), bf16),
+            pltpu.VMEM((3, 4, ORDER, PANEL), bf16),
             pltpu.VMEM(factor.shape, bf16),
             pltpu.VMEM(old_basis.shape, bf16),
             pltpu.VMEM(moment.shape, bf16),
-            pltpu.VMEM((8, PANEL), jnp.int32),
             pltpu.SMEM((8, PANEL), jnp.int32),
             pltpu.SemaphoreType.DMA((7,)),
             pltpu.SemaphoreType.DMA((2,)),
             pltpu.SemaphoreType.DMA((2,)),
             pltpu.SemaphoreType.DMA((3,)),
-            pltpu.SemaphoreType.DMA((2,)),
+            pltpu.SemaphoreType.DMA((2, 4)),
             pltpu.SemaphoreType.DMA,
-            pltpu.SemaphoreType.DMA((4,)),
+            pltpu.SemaphoreType.DMA((12,)),
         ],
         compiler_params=pltpu.CompilerParams(
             collective_id=0, has_side_effects=True, vmem_limit_bytes=60 * 2**20
         ),
         cost_estimate=pl.CostEstimate(flops=8 * 10**9, bytes_accessed=4 * 2**20, transcendentals=0),
     )(owner_table.reshape(1, BLOCKS), factor, old_basis, moment)
+    return pl.pallas_call(
+        place_kernel,
+        out_shape=(jax.ShapeDtypeStruct(moment.shape, bf16), kept),
+        in_specs=[pl.BlockSpec(memory_space=pltpu.SMEM), hbm, hbm],
+        out_specs=(hbm, hbm),
+        scratch_shapes=[
+            pltpu.VMEM(backs.shape, bf16),
+            pltpu.VMEM(bases.shape[1:], bf16),
+            pltpu.SemaphoreType.DMA((SHARES // 16 + 2 * SLOTS + 1,)),
+        ],
+        compiler_params=pltpu.CompilerParams(vmem_limit_bytes=60 * 2**20),
+    )(table, backs, bases)
 
 
 def solution(mesh):

time: 95.3 us -> 91.2 us (0.957)
  local copies, waits for them, and re-layouts: 3.22 us -> 0 us
    unnamed x4 -> x0, local copies, waits for them, and re-layouts: 3.22 us -> none
    pallas_call x1 -> x2, Pallas kernels: 91.3 us -> 90.4 us  [the longest x1 86.7 us: per_device(): pl.pallas_call(refresh_kernel, out_shape=(jax.ShapeDtypeStruct((2, SHARES...]
where the time goes in v5:
time: 91.2 us; the launch traced here: 91.1 us
  Pallas kernels  90.4 us (99%)
    pallas_call x1, Pallas kernels, per_device(): pl.pallas_call(refresh_kernel, out_shape=(jax.ShapeDtypeStruct((2, SHARES...  86.7 us
    pallas_call x1, Pallas kernels, per_device(): pl.pallas_call(place_kernel, out_shape=(jax.ShapeDtypeStruct(moment.shape...  3.73 us

profile of v5, /device:TPU:1, one launch (start us, length us, event | category | flops | bytes accessed | tf_op | source)
XLA Modules:
  0.0 91.1 jit_solution(9024954956196004955)
XLA Ops:
  0.6 86.7 %shard_map.59 = (bf16[2,64,16,256]{3,2,1,0:T(8,128)(2,1)}, bf16[1,2,512,512]{3,2,1,0:T(8,128)(2,1)}, s32[8,128]{1,0:T(8,128)}) custom-call(s32[1,56]{1,0:T(1,128)} %bitcast.1, bf16[56,8,512]{2,1,0:T(8,128)(2,1)} %factor_hbm.1, bf16[56,8,512]{2,1,0:T(8,128)(2,1)} %basis_hbm.1, bf16[56,16,512]{2,1,0:T(8,128)(2,1)} %moment_hbm.1), custom_call_target="tpu_custom_call" | custom-call | flops 8000000000 | bytes 4194304 | tf_op jit(solution)/shard_map/pallas_call | solution.py:654
  87.3 3.7 %shard_map.60 = (bf16[56,16,512]{2,1,0:T(8,128)(2,1)}, bf16[1,2,512,512]{3,2,1,0:T(8,128)(2,1)}) custom-call(s32[8,128]{1,0:T(8,128)} %get-tuple-element.5.table, bf16[2,64,16,256]{3,2,1,0:T(8,128)(2,1)} %get-tuple-element.6.backs, bf16[1,2,512,512]{3,2,1,0:T(8,128)(2,1)} %get-tuple-element.7.kept), custom_call_target="tpu_custom_call" | custom-call | tf_op jit(solution)/shard_map/pallas_call | solution.py:694

commit v6 on v5

--- a/solution.py
+++ b/solution.py
@@ -154,7 +154,7 @@
 
 
 def refresh_kernel(
-    owners,
+    owners_hbm,
     factor_hbm,
     basis_hbm,
     moment_hbm,
@@ -168,12 +168,12 @@
     got1,
     gotm,
     backs,
-    kept,
     old,
     work,
     diag,
     inverse,
     rots,
+    owners,
     factor,
     basis,
     moment,
@@ -189,15 +189,16 @@
     fetches = [
         pltpu.make_async_copy(src, dst, local.at[i])
         for i, (src, dst) in enumerate(
-            ((basis_hbm, basis), (factor_hbm, factor), (moment_hbm, moment))
+            (
+                (owners_hbm, owners),
+                (basis_hbm, basis),
+                (factor_hbm, factor),
+                (moment_hbm, moment),
+            )
         )
     ]
     for fetch in fetches:
         fetch.start()
-    stores = [
-        pltpu.make_async_copy(kept.at[slot], owner_basis.at[0, slot], local.at[4 + slot])
-        for slot in range(SLOTS)
-    ]
 
     me = lax.axis_index("fsdp") * 2 + lax.axis_index("own")
     panel = me // 16
@@ -223,10 +224,11 @@
 
     lax.fori_loop(1, SHARES, greet, 0)
 
+    fetches[0].wait()
     plan(owners, planned)
-    tables = pltpu.make_async_copy(planned, table, local.at[3])
+    tables = pltpu.make_async_copy(planned, table, local.at[4])
     tables.start()
-    for fetch in fetches[:2]:
+    for fetch in fetches[1:3]:
         fetch.wait()
     tables.wait()
 
@@ -383,8 +385,7 @@
 
     def keep(slot):
         there = jnp.full((ORDER, ORDER), table[3 + slot, me], jnp.int32)
-        kept[slot] = jnp.where(there > 0, work[:, ORDER:].T, 0.0).astype(jnp.bfloat16)
-        stores[slot].start()
+        owner_basis[0, slot] = jnp.where(there > 0, work[:, ORDER:].T, 0.0).astype(jnp.bfloat16)
 
     def turn(k):
         at = pl.multiple_of(k * PANEL, PANEL)
@@ -409,7 +410,7 @@
         return pltpu.make_async_copy(
             backs.at[half, FIRST[region] * 8 + seat],
             backr.at[half, hosts[region]],
-            local.at[6 + 2 * region + half],
+            local.at[5 + 2 * region + half],
         )
 
     def rotate(region, half, away):
@@ -488,7 +489,7 @@
     pl.semaphore_wait(barrier, SHARES - 1)
     post(0, pack0, send0, got0, recv0)
     post(1, pack1, send1, got1, recv1)
-    fetches[2].wait()
+    fetches[3].wait()
     post_moments()
 
     def step(i, _):
@@ -549,9 +550,6 @@
             took(region, False)
             for half in range(2):
                 local_reply(region, half).wait()
-
-    for store in stores:
-        store.wait()
 
     @pl.when(active[0])
     def _():
@@ -605,45 +603,27 @@
         planned[i:i + 1, :] = x[0:1, :]
 
 
-def place_kernel(table, backs, kept, moment_out, owner_basis, rows, bases, sems):
-    parts = SHARES // 16
-    loads, bases_in, bases_out = [], [], []
-    for q in range(parts):
-        cut = slice(16 * q, 16 * q + 16)
-        loads.append(pltpu.make_async_copy(backs.at[:, cut], rows.at[:, cut], sems.at[q]))
-        loads[q].start()
+def place_kernel(table, rows, bases, moment_out, owner_basis, sems):
+    keeps = []
     for slot in range(SLOTS):
-        bases_in.append(
-            pltpu.make_async_copy(kept.at[0, slot], bases.at[slot], sems.at[parts + slot])
+        keeps.append(
+            pltpu.make_async_copy(bases.at[0, slot], owner_basis.at[0, slot], sems.at[1 + slot])
         )
-        bases_out.append(
+        keeps[slot].start()
+
+    def place(b, _):
+        for half in range(2):
             pltpu.make_async_copy(
-                bases.at[slot], owner_basis.at[0, slot], sems.at[parts + SLOTS + slot]
-            )
-        )
-        bases_in[slot].start()
-
-    def place(t, _):
-        @pl.when(jnp.logical_not(is_idle(t)))
-        def _():
-            for half in range(2):
-                pltpu.make_async_copy(
-                    rows.at[half, t],
-                    moment_out.at[table[0, t], :, 2 * PANEL * half:2 * PANEL * (half + 1)],
-                    sems.at[parts + 2 * SLOTS],
-                ).start()
-
+                rows.at[half, table[2, b]],
+                moment_out.at[b, :, 2 * PANEL * half:2 * PANEL * (half + 1)],
+                sems.at[0],
+            ).start()
         return 0
 
-    for q in range(parts):
-        loads[q].wait()
-        lax.fori_loop(16 * q, 16 * q + 16, place, 0)
-    for slot in range(SLOTS):
-        bases_in[slot].wait()
-        bases_out[slot].start()
-    pltpu.make_async_copy(moment_out, moment_out, sems.at[parts + 2 * SLOTS]).wait()
-    for slot in range(SLOTS):
-        bases_out[slot].wait()
+    lax.fori_loop(0, BLOCKS, place, 0)
+    pltpu.make_async_copy(moment_out, moment_out, sems.at[0]).wait()
+    for keep in keeps:
+        keep.wait()
 
 
 def per_device(factor, old_basis, moment, owner_table):
@@ -651,6 +631,11 @@
     vmem = pl.BlockSpec(memory_space=pltpu.VMEM)
     hbm = pl.BlockSpec(memory_space=pl.ANY)
     kept = jax.ShapeDtypeStruct((1, SLOTS, ORDER, ORDER), bf16)
+    table = owner_table.reshape(1, BLOCKS)
+    held = [
+        pltpu.with_memory_space_constraint(x, pltpu.HBM)
+        for x in (table, factor, old_basis, moment)
+    ]
     backs, bases, table = pl.pallas_call(
         refresh_kernel,
         out_shape=(
@@ -658,8 +643,8 @@
             kept,
             jax.ShapeDtypeStruct((8, PANEL), jnp.int32),
         ),
-        in_specs=[vmem, hbm, hbm, hbm],
-        out_specs=(hbm, hbm, vmem),
+        in_specs=[hbm] * 4,
+        out_specs=(vmem, vmem, vmem),
         scratch_shapes=[
             pltpu.VMEM((SHARES, 8, WIDTHS[0][0]), bf16),
             pltpu.VMEM((SHARES, 8, WIDTHS[1][0]), bf16),
@@ -668,12 +653,12 @@
             pltpu.VMEM((SHARES, 8, WIDTHS[1][0]), bf16),
             pltpu.VMEM((72, 16, ORDER), bf16),
             pltpu.VMEM((2, 72, 16, 2 * PANEL), bf16),
-            pltpu.VMEM((SLOTS, ORDER, ORDER), bf16),
             pltpu.VMEM((ORDER, ORDER), bf16),
             pltpu.VMEM((ORDER, 2 * ORDER), jnp.float32),
             pltpu.VMEM((PANEL, PANEL), jnp.float32),
             pltpu.VMEM((PANEL, PANEL), jnp.float32),
             pltpu.VMEM((3, 4, ORDER, PANEL), bf16),
+            pltpu.VMEM(table.shape, jnp.int32),
             pltpu.VMEM(factor.shape, bf16),
             pltpu.VMEM(old_basis.shape, bf16),
             pltpu.VMEM(moment.shape, bf16),
@@ -687,21 +672,17 @@
             pltpu.SemaphoreType.DMA((12,)),
         ],
         compiler_params=pltpu.CompilerParams(
-            collective_id=0, has_side_effects=True, vmem_limit_bytes=60 * 2**20
+            collective_id=0, has_side_effects=True, vmem_limit_bytes=40 * 2**20
         ),
         cost_estimate=pl.CostEstimate(flops=8 * 10**9, bytes_accessed=4 * 2**20, transcendentals=0),
-    )(owner_table.reshape(1, BLOCKS), factor, old_basis, moment)
+    )(*held)
     return pl.pallas_call(
         place_kernel,
         out_shape=(jax.ShapeDtypeStruct(moment.shape, bf16), kept),
-        in_specs=[pl.BlockSpec(memory_space=pltpu.SMEM), hbm, hbm],
+        in_specs=[pl.BlockSpec(memory_space=pltpu.SMEM), vmem, vmem],
         out_specs=(hbm, hbm),
-        scratch_shapes=[
-            pltpu.VMEM(backs.shape, bf16),
-            pltpu.VMEM(bases.shape[1:], bf16),
-            pltpu.SemaphoreType.DMA((SHARES // 16 + 2 * SLOTS + 1,)),
-        ],
-        compiler_params=pltpu.CompilerParams(vmem_limit_bytes=60 * 2**20),
+        scratch_shapes=[pltpu.SemaphoreType.DMA((1 + SLOTS,))],
+        compiler_params=pltpu.CompilerParams(vmem_limit_bytes=16 * 2**20),
     )(table, backs, bases)
 
 

time: 91.2 us -> 88.5 us (0.970)
  Pallas kernels: 90.4 us -> 87.7 us
    pallas_call x1, Pallas kernels: 3.73 us -> 1.98 us  [per_device(): pl.pallas_call(place_kernel, out_shape=(jax.ShapeDtypeStruct(moment.shape...]
    pallas_call x1, Pallas kernels: 86.7 us -> 85.7 us  [per_device(): pl.pallas_call(refresh_kernel, out_shape=(jax.ShapeDtypeStruct((2, SHARES...]
where the time goes in v6:
time: 88.5 us; the launch traced here: 88.3 us
  Pallas kernels  87.7 us (99%)
    pallas_call x1, Pallas kernels, per_device(): pl.pallas_call(refresh_kernel, out_shape=(jax.ShapeDtypeStruct((2, SHARES...  85.7 us
    pallas_call x1, Pallas kernels, per_device(): pl.pallas_call(place_kernel, out_shape=(jax.ShapeDtypeStruct(moment.shape...  1.98 us

profile of v6, /device:TPU:1, one launch (start us, length us, event | category | flops | bytes accessed | tf_op | source)
XLA Modules:
  0.0 88.3 jit_solution(14160854370919026077)
XLA Ops:
  0.6 85.7 %shard_map.59 = (bf16[2,64,16,256]{3,2,1,0:T(8,128)(2,1)S(1)}, bf16[1,2,512,512]{3,2,1,0:T(8,128)(2,1)S(1)}, s32[8,128]{1,0:T(8,128)S(1)}) custom-call(s32[1,56]{1,0:T(1,128)} %bitcast.1, bf16[56,8,512]{2,1,0:T(8,128)(2,1)} %factor_hbm.1, bf16[56,8,512]{2,1,0:T(8,128)(2,1)} %basis_hbm.1, bf16[56,16,512]{2,1,0:T(8,128)(2,1)} %moment_hbm.1), custom_call_target="tpu_custom_call" | custom-call | flops 8000000000 | bytes 4194304 | tf_op jit(solution)/shard_map/pallas_call | solution.py:639
  86.4 2.0 %shard_map.60 = (bf16[56,16,512]{2,1,0:T(8,128)(2,1)}, bf16[1,2,512,512]{3,2,1,0:T(8,128)(2,1)}) custom-call(s32[8,128]{1,0:T(8,128)S(1)} %get-tuple-element.5.table, bf16[2,64,16,256]{3,2,1,0:T(8,128)(2,1)S(1)} %get-tuple-element.6.rows, bf16[1,2,512,512]{3,2,1,0:T(8,128)(2,1)S(1)} %get-tuple-element.7.bases), custom_call_target="tpu_custom_call" | custom-call | tf_op jit(solution)/shard_map/pallas_call | solution.py:679

commit v7 on v6

--- a/solution.py
+++ b/solution.py
@@ -507,7 +507,7 @@
 
         for half in range(2):
 
-            @pl.when(i == 5 + half)
+            @pl.when(i == 6)
             def _():
                 rotate_half(half)
 

time: 88.5 us -> 88.2 us (level); the launches traced: 88.3 us -> 87.1 us
  Pallas kernels: 87.7 us -> 86.5 us
    pallas_call x1, Pallas kernels: 85.7 us -> 84.5 us  [per_device(): pl.pallas_call(refresh_kernel, out_shape=(jax.ShapeDtypeStruct((2, SHARES...]
where the time goes in v7:
time: 88.2 us; the launch traced here: 87.1 us
  Pallas kernels  86.5 us (98%)
    pallas_call x1, Pallas kernels, per_device(): pl.pallas_call(refresh_kernel, out_shape=(jax.ShapeDtypeStruct((2, SHARES...  84.5 us
    pallas_call x1, Pallas kernels, per_device(): pl.pallas_call(place_kernel, out_shape=(jax.ShapeDtypeStruct(moment.shape...  1.98 us

profile of v7, /device:TPU:1, one launch (start us, length us, event | category | flops | bytes accessed | tf_op | source)
XLA Modules:
  0.0 87.1 jit_solution(18008164712036155785)
XLA Ops:
  0.6 84.5 %shard_map.59 = (bf16[2,64,16,256]{3,2,1,0:T(8,128)(2,1)S(1)}, bf16[1,2,512,512]{3,2,1,0:T(8,128)(2,1)S(1)}, s32[8,128]{1,0:T(8,128)S(1)}) custom-call(s32[1,56]{1,0:T(1,128)} %bitcast.1, bf16[56,8,512]{2,1,0:T(8,128)(2,1)} %factor_hbm.1, bf16[56,8,512]{2,1,0:T(8,128)(2,1)} %basis_hbm.1, bf16[56,16,512]{2,1,0:T(8,128)(2,1)} %moment_hbm.1), custom_call_target="tpu_custom_call" | custom-call | flops 8000000000 | bytes 4194304 | tf_op jit(solution)/shard_map/pallas_call | solution.py:639
  85.1 2.0 %shard_map.60 = (bf16[56,16,512]{2,1,0:T(8,128)(2,1)}, bf16[1,2,512,512]{3,2,1,0:T(8,128)(2,1)}) custom-call(s32[8,128]{1,0:T(8,128)S(1)} %get-tuple-element.5.table, bf16[2,64,16,256]{3,2,1,0:T(8,128)(2,1)S(1)} %get-tuple-element.6.rows, bf16[1,2,512,512]{3,2,1,0:T(8,128)(2,1)S(1)} %get-tuple-element.7.bases), custom_call_target="tpu_custom_call" | custom-call | tf_op jit(solution)/shard_map/pallas_call | solution.py:679
